TPU v7x, 256 devices: a whole 4x4x8 slice. The times are simulated.
256 devices in a mesh: blk: 128 (over z, x, y_hi, core), span: 2 (over y_lo).
Axes of the slice: x: 4, y: 4 (y_hi: 2, y_lo: 2; y = y_hi * 2 + y_lo), z: 8, core: 2. Of those that a mesh axis runs over, the one named last changes fastest.
Arguments:
- theta_init: float32 [128, 16, 128, 256], P('blk', None, None, 'span'), may hold values from -5 to 5
- conductivity: float32 [128, 16, 128, 256], P('blk', None, None, 'span'), may hold values from 0.03 to 0.14
- velocity: float32 [128, 3, 16, 128, 256], P('blk', None, None, None, 'span'), may hold values from -0.05 to 0.05
- heat_source: float32 [128, 16, 128, 256], P('blk', None, None, 'span'), may hold values from -0.25 to 0.25
- wall_init: float32 [128, 128, 256], P('blk', None, 'span'), may hold values from -1.5 to 1.5
- block_type: int32 [128], replicated, may hold values from 0 to 1, as said below
- partner_block: int32 [128, 128], P('blk'), may hold values from 0 to 127, as said below
- partner_row: int32 [128, 128], P('blk'), may hold values from 0 to 127
Outputs:
- temperature: float32 [128, 16, 128, 256], P('blk', None, None, 'span')
- wall_row: float32 [128, 128, 256], P('blk', None, 'span')
Inputs may be any that keep to these rules, and one draw needn't show every extreme that they name: `block_type`: exactly 64 blocks are fluid. `partner_block`: the partner block is always of the other type and the matching is mutual: the partner row's partner is the row itself; each block has exactly 2 wall rows that face each block of the other type.
All inputs are finite; a program needn't handle non-finite values.
Results may differ from a plain program's by a relative error of at most 0.0003.
Values sent between devices are 32-bit elements; how exact they have to be, the bound alone decides.
A program may use at most 128 MiB of HBM per device.

v0:
```python
import functools

import jax
import jax.numpy as jnp
from jax import lax
from jax.experimental import pallas as pl
from jax.experimental.pallas import tpu as pltpu
from jax.sharding import PartitionSpec as P

MESH = pl.DeviceIdType.MESH
SWEEPS = 3
CY, CX, LZ = 16, 128, 128
TILES = CX // 8 + 1
ROWS = 8 * TILES
PAD = ROWS + 16
F32 = jnp.float32
AW, AE, AS, AN, AB, AA, AD, SRC = range(8)


def tile(i, shift=0):
    return pl.ds(8 + 8 * i + shift, 8)


def row8(i):
    return pl.ds(8 * i, 8)


def remote(src, dst, send, recv, device):
    return pltpu.make_async_remote_copy(
        src_ref=src, dst_ref=dst, send_sem=send, recv_sem=recv, device_id=device, device_id_type=MESH
    )


def split3(x):
    hi = x.astype(jnp.bfloat16)
    rest = x - hi.astype(F32)
    mid = rest.astype(jnp.bfloat16)
    low = (rest - mid.astype(F32)).astype(jnp.bfloat16)
    return hi, mid, low


def pick(chooser, x):
    return sum(jnp.dot(chooser, part, preferred_element_type=F32) for part in split3(x))


def kernel(
    n, theta_ref, cond_ref, vel_ref, heat_ref, wall_ref, kind_ref, block_ref, row_ref,
    theta_out, wall_out,
    th, kb, vb, hb, co, st, sk, sv, sco, sw, pz,
    xs, xr, qs, qr, cr, wx, wp, wc, tr, q1, q1r, c1r,
    sb, rb, choose_send, choose_recv,
    load_sem, send_sem, recv_sem, many_send, many_recv,
):
    b, s = lax.axis_index("blk"), lax.axis_index("span")
    chunk = 2 * CX // n
    east, west = lax.rem(b + 1, n), lax.rem(b + n - 1, n)
    E, W, Z, ZE, ZW = (east, s), (west, s), (b, 1 - s), (east, 1 - s), (west, 1 - s)

    loads = [
        pltpu.make_async_copy(theta_ref.at[0], th.at[0, pl.ds(1, CY), pl.ds(8, CX)], load_sem.at[0]),
        pltpu.make_async_copy(cond_ref.at[0], kb.at[:, pl.ds(8, CX)], load_sem.at[1]),
        pltpu.make_async_copy(vel_ref.at[0], vb.at[:, :, pl.ds(0, CX)], load_sem.at[2]),
        pltpu.make_async_copy(heat_ref.at[0], hb.at[:, pl.ds(0, CX)], load_sem.at[3]),
        pltpu.make_async_copy(wall_ref.at[0], th.at[0, 0, pl.ds(8, CX)], load_sem.at[4]),
    ]
    for load in loads:
        load.start()

    rb[:, pl.ds(b, 1)] = jnp.zeros((2, 1, chunk, LZ), F32)

    barrier = pltpu.get_barrier_semaphore()

    def greet(d, carry):
        pl.semaphore_signal(barrier, inc=1, device_id=(lax.rem(b + d, n), s), device_id_type=MESH)
        return carry

    lax.fori_loop(1, n, greet, 0)
    for peer in (Z, ZE, ZW):
        pl.semaphore_signal(barrier, inc=1, device_id=peer, device_id_type=MESH)

    fluid = kind_ref[b].astype(F32)
    metal = 1.0 - fluid
    same_west = 1.0 - jnp.abs(kind_ref[west].astype(F32) - fluid)
    same_east = 1.0 - jnp.abs(kind_ref[east].astype(F32) - fluid)

    lane = lax.broadcasted_iota(jnp.int32, (8, LZ), 1)
    sub = lax.broadcasted_iota(jnp.int32, (8, LZ), 0)
    group, place = lane // 8, lane % 8
    first_lane, last_lane = lane == 0, lane == LZ - 1
    low_half = place < 4
    middle = (place >= 2) & (place < 6)

    mine = jnp.broadcast_to(block_ref[...].astype(F32), (CX, CX))
    theirs = jnp.broadcast_to(row_ref[...].astype(F32), (CX, CX))
    mine_t, theirs_t = mine.T, theirs.T
    at_row = lax.broadcasted_iota(jnp.int32, (CX, CX), 0)
    at_col = lax.broadcasted_iota(jnp.int32, (CX, CX), 1)
    alike = mine_t == mine
    rank = jnp.sum(jnp.where(alike & (at_row < at_col), 1.0, 0.0), axis=0, keepdims=True)
    code = (chunk * mine[0:1] + rank).astype(jnp.int32)
    choose_send[...] = jnp.where(
        lax.broadcasted_iota(jnp.int32, (2 * CX, CX), 0) == code, 1.0, 0.0
    ).astype(jnp.bfloat16)
    rank_t = jnp.sum(jnp.where(alike & (theirs < theirs_t), 1.0, 0.0), axis=1, keepdims=True)
    code_t = (chunk * mine_t[:, 0:1] + rank_t).astype(jnp.int32)
    choose_recv[...] = jnp.where(
        lax.broadcasted_iota(jnp.int32, (CX, 2 * CX), 1) == code_t, 1.0, 0.0
    ).astype(jnp.bfloat16)

    for p in range(2):
        th[p, CY + 1] = jnp.zeros((PAD, LZ), F32)

    for load in loads:
        load.wait()

    def edges(load):
        out = pltpu.roll(load(0), 4, 1)
        for y in range(1, CY):
            out = jnp.where(group == y, pltpu.roll(load(y), (8 * y + 4) % LZ, 1), out)
        return out

    def pack_six(i, at, at_pad):
        q_th = edges(lambda y: th[0, y + 1, at_pad])
        q_k = edges(lambda y: kb[y, at_pad])
        q_v = [edges(lambda y, d=d: vb[d, y, at]) for d in range(3)]
        q_h = edges(lambda y: hb[y, at])
        return (
            q_th,
            q_k,
            jnp.where(middle, q_v[0], pltpu.roll(q_v[1], 4, 1)),
            jnp.where(middle, q_v[2], pltpu.roll(q_h, 4, 1)),
        )

    def pack_tile(i, carry):
        at = pl.ds(pl.multiple_of(8 * i, 8), 8)
        at_pad = pl.ds(pl.multiple_of(8 * i + 8, 8), 8)
        for slot, q in enumerate(pack_six(i, at, at_pad)):
            qs[slot, at] = q
        return carry

    lax.fori_loop(0, TILES - 1, pack_tile, 0)

    def pack_rows(y, carry):
        last, pad_last = pl.ds(CX - 8, 8), pl.ds(CX, 8)
        xs[0, 0, y] = jnp.where(sub >= 5, th[0, y + 1, pad_last], pltpu.roll(kb[y, pad_last], 5, 0))
        xs[0, 1, y] = jnp.where(
            sub >= 6,
            vb[0, y, last],
            jnp.where(
                sub >= 4,
                pltpu.roll(vb[1, y, last], 6, 0),
                jnp.where(sub >= 2, pltpu.roll(vb[2, y, last], 4, 0), pltpu.roll(hb[y, last], 2, 0)),
            ),
        )
        zero, pad_zero = pl.ds(0, 8), pl.ds(8, 8)
        xs[1, 0, y] = jnp.where(sub < 3, th[0, y + 1, pad_zero], pltpu.roll(kb[y, pad_zero], 3, 0))
        xs[1, 1, y] = jnp.where(
            sub < 2,
            vb[0, y, zero],
            jnp.where(
                sub < 4,
                pltpu.roll(vb[1, y, zero], 2, 0),
                jnp.where(sub < 6, pltpu.roll(vb[2, y, zero], 4, 0), pltpu.roll(hb[y, zero], 6, 0)),
            ),
        )
        return carry

    lax.fori_loop(0, CY, pack_rows, 0)

    pl.semaphore_wait(barrier, n + 2)

    def wall_copies(r, plane, base):
        tail, head = plane.at[pl.ds(CX, 8)], plane.at[pl.ds(8, 8)]
        return [
            remote(tail, wx.at[r, 0], send_sem.at[base], recv_sem.at[base], E),
            remote(head, wx.at[r, 1], send_sem.at[base + 1], recv_sem.at[base + 1], W),
            remote(plane.at[pl.ds(8, CX)], wp.at[r], send_sem.at[base + 2], recv_sem.at[base + 2], Z),
            remote(tail, wc.at[r, 0], send_sem.at[base + 3], recv_sem.at[base + 3], ZE),
            remote(head, wc.at[r, 1], send_sem.at[base + 4], recv_sem.at[base + 4], ZW),
        ]

    copies = [
        remote(xs.at[0], xr.at[0], send_sem.at[0], recv_sem.at[0], E),
        remote(xs.at[1], xr.at[1], send_sem.at[1], recv_sem.at[1], W),
        remote(qs.at[:, pl.ds(CX - 8, 8)], cr.at[0], send_sem.at[3], recv_sem.at[3], ZE),
        remote(qs.at[:, pl.ds(0, 8)], cr.at[1], send_sem.at[4], recv_sem.at[4], ZW),
        remote(qs, qr, send_sem.at[2], recv_sem.at[2], Z),
    ] + wall_copies(0, th.at[0, 0], 5)
    for copy in copies:
        copy.start()
    for copy in copies:
        copy.wait()

    last = TILES - 1
    rows_last = row8(last)

    def unpack_rows(y, carry):
        e0, e1, w0, w1 = xr[1, 0, y], xr[1, 1, y], xr[0, 0, y], xr[0, 1, y]
        near = sub < 4
        t = jnp.where(near, e0, w0)
        th[0, y + 1, tile(last)] = t
        th[0, y + 1, tile(-1)] = t
        th[0, y + 1, tile(TILES)] = th[0, y + 1, tile(0)]
        k = jnp.where(near, pltpu.roll(e0, 5, 0), pltpu.roll(w0, 3, 0))
        kb[y, tile(last)] = k
        kb[y, tile(-1)] = k
        kb[y, tile(TILES)] = kb[y, tile(0)]
        vb[0, y, rows_last] = jnp.where(near, e1, w1)
        vb[1, y, rows_last] = jnp.where(near, pltpu.roll(e1, 6, 0), pltpu.roll(w1, 2, 0))
        vb[2, y, rows_last] = jnp.where(near, pltpu.roll(e1, 4, 0), pltpu.roll(w1, 4, 0))
        hb[y, rows_last] = jnp.where(near, pltpu.roll(e1, 2, 0), pltpu.roll(w1, 6, 0))
        return carry

    lax.fori_loop(0, CY, unpack_rows, 0)

    def put_strip(ref, i, own, other):
        for side in range(2):
            value = jnp.where(low_half, other, own) if side == 0 else jnp.where(low_half, own, other)
            ref[side, tile(i)] = value
            if i == last:
                ref[side, tile(-1)] = value
            if i == 0:
                ref[side, tile(TILES)] = value

    def strip_wall(r, p):
        th[p, 0, tile(last)] = jnp.where(sub < 4, wx[r, 1], wx[r, 0])
        th[1 - p, 0, pl.ds(8, ROWS)] = th[p, 0, pl.ds(8, ROWS)]
        for i in range(TILES):
            own = pltpu.roll(th[p, 0, tile(i)], 4, 1)
            other = wp[r, row8(i)] if i < last else jnp.where(sub < 4, wc[r, 1], wc[r, 0])
            other = pltpu.roll(other, 4, 1)
            sw[0, row8(i)] = jnp.where(low_half, other, own)
            sw[1, row8(i)] = jnp.where(low_half, own, other)

    halo_q = pack_six(last, rows_last, tile(last))
    for i in range(TILES):
        own = [qs[slot, row8(i)] for slot in range(4)] if i < last else halo_q
        other = [
            qr[slot, row8(i)] if i < last else jnp.where(sub < 4, cr[1, slot], cr[0, slot])
            for slot in range(4)
        ]
        put_strip(st.at[0], i, own[0], other[0])
        put_strip(sk, i, own[1], other[1])
        for slot in (2, 3):
            for part in range(2):
                o, t = own[slot], other[slot]
                if part:
                    o, t = pltpu.roll(o, LZ - 4, 1), pltpu.roll(t, LZ - 4, 1)
                at = 2 * (slot - 2) + part
                sv[at, 0, row8(i)] = jnp.where(low_half, t, o)
                sv[at, 1, row8(i)] = jnp.where(low_half, o, t)
    strip_wall(0, 0)

    def face_masks(i, a_w, a_e):
        if i == 0:
            a_w = jnp.where(sub == 0, same_west * a_w, a_w)
        if i == last - 1:
            a_e = jnp.where(sub == 7, same_east * a_e, a_e)
        return a_w, a_e

    def coefficients(k, k_w, k_e, k_s, k_n, k_b, k_a, v, i, bottom, top):
        v = [fluid * x for x in v]
        a_w = 0.5 * (k + k_w) + jnp.maximum(v[0], 0.0)
        a_e = 0.5 * (k + k_e) - jnp.minimum(v[0], 0.0)
        a_w, a_e = face_masks(i, a_w, a_e)
        a_b = 0.5 * (k + k_b) + jnp.maximum(v[1], 0.0)
        a_b = a_b * (1.0 - metal * bottom)
        a_a = (0.5 * (k + k_a) - jnp.minimum(v[1], 0.0)) * (1.0 - top)
        a_s = 0.5 * (k + k_s) + jnp.maximum(v[2], 0.0)
        a_n = 0.5 * (k + k_n) - jnp.minimum(v[2], 0.0)
        a_d = 1.0 - (a_w + a_e + a_s + a_n + a_b + a_a)
        return a_w, a_e, a_s, a_n, a_b + metal * bottom, a_a, a_d

    strip_bottom = (group == 0).astype(F32)
    strip_top = (group == CY - 1).astype(F32)
    for side in range(2):
        for i in range(TILES):
            k = sk[side, tile(i)]
            k_b = jnp.where(group == 0, k, pltpu.roll(k, 8, 1))
            a = coefficients(
                k, sk[side, tile(i, -1)], sk[side, tile(i, 1)], pltpu.roll(k, 1, 1), pltpu.roll(k, LZ - 1, 1),
                k_b, pltpu.roll(k, LZ - 8, 1), [sv[d, side, row8(i)] for d in range(3)], i, strip_bottom, strip_top,
            )
            for slot, value in enumerate(a):
                sco[slot, side, row8(i)] = value
            sco[SRC, side, row8(i)] = sv[3, side, row8(i)]

    def join(ref):
        for i in range(TILES):
            pz[row8(i)] = jnp.where(place == 3, ref[0, tile(i)], ref[1, tile(i)])

    join(sk)

    def span_neighbours(c, z, y):
        z = pltpu.roll(z, 124 - 8 * y, 1)
        return (
            pltpu.roll(jnp.where(last_lane, z, c), 1, 1),
            pltpu.roll(jnp.where(first_lane, z, c), LZ - 1, 1),
        )

    def plane_coefficients(y, carry):
        bottom = (y == 0).astype(F32)
        top = (y == CY - 1).astype(F32)
        below, above = jnp.maximum(y - 1, 0), jnp.minimum(y + 1, CY - 1)
        for i in range(TILES):
            k = kb[y, tile(i)]
            k_s, k_n = span_neighbours(k, pz[row8(i)], y)
            a = coefficients(
                k, kb[y, tile(i, -1)], kb[y, tile(i, 1)], k_s, k_n, kb[below, tile(i)], kb[above, tile(i)],
                [vb[d, y, row8(i)] for d in range(3)], i, bottom, top,
            )
            for slot, value in enumerate(a):
                co[slot, y, row8(i)] = value
        return carry

    lax.fori_loop(0, CY, plane_coefficients, 0)

    def sweep(p):
        join(st.at[p])

        def plane(y, carry):
            for i in range(TILES):
                at = row8(i)
                c = th[p, y + 1, tile(i)]
                south, north = span_neighbours(c, pz[at], y)
                new = (
                    (hb[y, at] + co[AD, y, at] * c)
                    + (co[AW, y, at] * th[p, y + 1, tile(i, -1)] + co[AE, y, at] * th[p, y + 1, tile(i, 1)])
                    + (co[AS, y, at] * south + co[AN, y, at] * north)
                    + (co[AB, y, at] * th[p, y, tile(i)] + co[AA, y, at] * th[p, y + 2, tile(i)])
                )
                th[1 - p, y + 1, tile(i)] = new
                if i == last:
                    th[1 - p, y + 1, tile(-1)] = new
                if i == 0:
                    th[1 - p, y + 1, tile(TILES)] = new
            return carry

        lax.fori_loop(0, CY, plane, 0)
        for side in range(2):
            for i in range(TILES):
                at = row8(i)
                c = st[p, side, tile(i)]
                below = jnp.where(group == 0, sw[side, at], pltpu.roll(c, 8, 1))
                a = [sco[slot, side, at] for slot in range(8)]
                new = (
                    (a[SRC] + a[AD] * c)
                    + (a[AW] * st[p, side, tile(i, -1)] + a[AE] * st[p, side, tile(i, 1)])
                    + (a[AS] * pltpu.roll(c, 1, 1) + a[AN] * pltpu.roll(c, LZ - 1, 1))
                    + (a[AB] * below + a[AA] * pltpu.roll(c, LZ - 8, 1))
                )
                st[1 - p, side, tile(i)] = new
                if i == last:
                    st[1 - p, side, tile(-1)] = new
                if i == 0:
                    st[1 - p, side, tile(TILES)] = new

    own = pl.ds(8, CX)

    def send_faces(r, p):
        field, wall = th[p, 1, own], th[p, 0, own]
        sent = fluid * (kb[0, own] * (field - wall)) + metal * field
        sb[...] = pick(choose_send[...], sent).reshape(n, chunk, LZ)

        def to(zd, i):
            x, y, c = (b // 4) % 4 + 3 - i // 4, (b // 2) % 2 + 1 - (i // 2) % 2, b % 2 + 1 - i % 2
            z = lax.rem(b // 16 + zd, n // 16)
            t = z * 16 + lax.rem(x, 4) * 4 + lax.rem(y, 2) * 2 + lax.rem(c, 2)
            remote(sb.at[t], rb.at[r, b], many_send.at[r], many_recv.at[r], (t, s)).start()

        for zd in (4, 3, 5, 2, 6, 1, 7):
            if zd < n // 16:
                lax.fori_loop(0, 16, lambda i, carry, zd=zd: (to(zd, i), carry)[1], 0)
        lax.fori_loop(0, 15, lambda i, carry: (to(0, i), carry)[1], 0)

    def receive_faces(r):
        others = pl.ds(0, n - 1)
        remote(sb.at[others], rb.at[r, others], many_send.at[r], many_recv.at[r], Z).wait()
        return pick(choose_recv[...], rb[r].reshape(2 * CX, LZ))

    p = 0
    for _ in range(SWEEPS):
        sweep(p)
        p = 1 - p
    send_faces(0, p)

    def pack_theta(i, carry):
        at_pad = pl.ds(pl.multiple_of(8 * i + 8, 8), 8)
        q1[pl.ds(pl.multiple_of(8 * i, 8), 8)] = edges(lambda y: th[p, y + 1, at_pad])
        return carry

    lax.fori_loop(0, TILES - 1, pack_theta, 0)
    planes = pl.ds(1, CY)
    copies = [
        remote(th.at[p, planes, pl.ds(CX, 8)], tr.at[0], send_sem.at[10], recv_sem.at[10], E),
        remote(th.at[p, planes, pl.ds(8, 8)], tr.at[1], send_sem.at[11], recv_sem.at[11], W),
        remote(q1.at[pl.ds(CX - 8, 8)], c1r.at[0], send_sem.at[12], recv_sem.at[12], ZE),
        remote(q1.at[pl.ds(0, 8)], c1r.at[1], send_sem.at[13], recv_sem.at[13], ZW),
        remote(q1, q1r, send_sem.at[14], recv_sem.at[14], Z),
    ]
    for copy in copies:
        copy.start()
    for copy in copies:
        copy.wait()

    def unpack_theta(y, carry):
        t = jnp.where(sub < 4, tr[1, y], tr[0, y])
        th[p, y + 1, tile(last)] = t
        th[p, y + 1, tile(-1)] = t
        return carry

    lax.fori_loop(0, CY, unpack_theta, 0)
    halo_th = edges(lambda y: th[p, y + 1, tile(last)])
    for i in range(TILES):
        own_q = q1[row8(i)] if i < last else halo_th
        other_q = q1r[row8(i)] if i < last else jnp.where(sub < 4, c1r[1], c1r[0])
        put_strip(st.at[p], i, own_q, other_q)

    th[p, 0, own] = receive_faces(0)
    copies = wall_copies(1, th.at[p, 0], 15)
    for copy in copies:
        copy.start()
    for copy in copies:
        copy.wait()
    strip_wall(1, p)
    for _ in range(SWEEPS):
        sweep(p)
        p = 1 - p
    send_faces(1, p)
    store = pltpu.make_async_copy(th.at[p, planes, own], theta_out.at[0], load_sem.at[0])
    store.start()
    wall_out[0] = receive_faces(1)
    store.wait()


def solution(mesh):
    n = mesh.shape["blk"]
    chunk = 2 * CX // n

    def part(theta, cond, vel, heat, wall, kinds, blocks, rows):
        hbm = pl.BlockSpec(memory_space=pl.ANY)
        vmem = pl.BlockSpec(memory_space=pltpu.VMEM)
        buf = lambda *shape: pltpu.VMEM(shape, F32)
        return pl.pallas_call(
            functools.partial(kernel, n),
            out_shape=(
                jax.ShapeDtypeStruct(theta.shape, F32),
                jax.ShapeDtypeStruct(wall.shape, F32),
            ),
            in_specs=[hbm] * 5 + [pl.BlockSpec(memory_space=pltpu.SMEM), vmem, vmem],
            out_specs=(hbm, vmem),
            scratch_shapes=[
                buf(2, CY + 2, PAD, LZ),
                buf(CY, PAD, LZ),
                buf(3, CY, ROWS, LZ),
                buf(CY, ROWS, LZ),
                buf(7, CY, ROWS, LZ),
                buf(2, 2, PAD, LZ),
                buf(2, PAD, LZ),
                buf(4, 2, ROWS, LZ),
                buf(8, 2, ROWS, LZ),
                buf(2, ROWS, LZ),
                buf(ROWS, LZ),
                buf(2, 2, CY, 8, LZ),
                buf(2, 2, CY, 8, LZ),
                buf(4, CX, LZ),
                buf(4, CX, LZ),
                buf(2, 4, 8, LZ),
                buf(2, 2, 8, LZ),
                buf(2, CX, LZ),
                buf(2, 2, 8, LZ),
                buf(2, CY, 8, LZ),
                buf(CX, LZ),
                buf(CX, LZ),
                buf(2, 8, LZ),
                buf(n, chunk, LZ),
                buf(2, n, chunk, LZ),
                pltpu.VMEM((2 * CX, CX), jnp.bfloat16),
                pltpu.VMEM((CX, 2 * CX), jnp.bfloat16),
                pltpu.SemaphoreType.DMA((5,)),
                pltpu.SemaphoreType.DMA((20,)),
                pltpu.SemaphoreType.DMA((20,)),
                pltpu.SemaphoreType.DMA((2,)),
                pltpu.SemaphoreType.DMA((2,)),
            ],
            compiler_params=pltpu.CompilerParams(
                collective_id=0, has_side_effects=True, vmem_limit_bytes=48 * 2**20
            ),
        )(theta, cond, vel, heat, wall, kinds, blocks, rows)

    whole = P("blk", None, None, "span")
    rows = P("blk", None, "span")
    return jax.shard_map(
        part,
        mesh=mesh,
        in_specs=(whole, whole, P("blk", None, None, None, "span"), whole, rows, P(), P("blk", None), P("blk", None)),
        out_specs=(whole, rows),
        check_vma=False,
    )
```

profile of v0, /device:TPU:1, one launch (start us, length us, event | category | flops | bytes accessed | tf_op | source)
XLA Modules:
  0.0 82.9 jit_solution(12492108564081297493)
XLA Ops:
  0.6 0.0 copy-start
  0.6 1.2 %copy-done = f32[1,16,128,128]{3,2,1,0:T(8,128)S(1)} copy-done((f32[1,16,128,128]{3,2,1,0:T(8,128)S(1)}, f32[1,16,128,128]{3,2,1,0:T(8,128)}, u32[]{:S(2)}) %copy-start) | copy-done | bytes 1048600
  1.9 0.0 copy-start.1
  1.9 1.2 %copy-done.1 = f32[1,16,128,128]{3,2,1,0:T(8,128)S(1)} copy-done((f32[1,16,128,128]{3,2,1,0:T(8,128)S(1)}, f32[1,16,128,128]{3,2,1,0:T(8,128)}, u32[]{:S(2)}) %copy-start.1) | copy-done | bytes 1048600
  3.1 0.0 copy-start.2
  3.1 1.2 %copy-done.2 = f32[1,16,128,128]{3,2,1,0:T(8,128)S(1)} copy-done((f32[1,16,128,128]{3,2,1,0:T(8,128)S(1)}, f32[1,16,128,128]{3,2,1,0:T(8,128)}, u32[]{:S(2)}) %copy-start.2) | copy-done | bytes 1048600
  4.3 0.0 copy-start.3
  4.3 0.8 %copy-done.3 = f32[1,128,128]{2,1,0:T(8,128)S(1)} copy-done((f32[1,128,128]{2,1,0:T(8,128)S(1)}, f32[1,128,128]{2,1,0:T(8,128)}, u32[]{:S(2)}) %copy-start.3) | copy-done | bytes 65560
  5.1 0.0 copy-start.4
  5.2 0.7 copy-done.4
  5.8 0.0 copy-start.5
  5.8 0.7 copy-done.5
  6.5 0.0 copy-start.6
  6.5 0.7 copy-done.6
  7.1 74.1 %shard_map.95 = (f32[1,16,128,128]{3,2,1,0:T(8,128)S(1)}, f32[1,128,128]{2,1,0:T(8,128)S(1)}) custom-call(f32[1,16,128,128]{3,2,1,0:T(8,128)S(1)} %copy-done, f32[1,16,128,128]{3,2,1,0:T(8,128)S(1)} %copy-done.1, f32[1,3,16,128,128]{4,3,2,1,0:T(8,128)} %vel_ref.1, f32[1,16,128,128]{3,2,1,0:T(8,128)S(1)} %copy-done.2, f32[1,128,128]{2,1,0:T(8,128)S(1)} %copy-done.3, ...), custom_call_target="tpu_custom_call" | custom-call | tf_op jit(solution)/shard_map/pallas_call | solution.py:444
  81.3 1.0 %copy.12 = f32[1,16,128,128]{3,2,1,0:T(8,128)} copy(f32[1,16,128,128]{3,2,1,0:T(8,128)S(1)} %get-tuple-element.4) | data formatting | bytes 2097152
  82.2 0.6 copy.13
Async XLA Ops:
  0.6 1.2 %copy-start = (f32[1,16,128,128]{3,2,1,0:T(8,128)S(1)}, f32[1,16,128,128]{3,2,1,0:T(8,128)}, u32[]{:S(2)}) copy-start(f32[1,16,128,128]{3,2,1,0:T(8,128)} %theta_ref.1) | copy-start | bytes 3145732
  1.9 1.2 %copy-start.1 = (f32[1,16,128,128]{3,2,1,0:T(8,128)S(1)}, f32[1,16,128,128]{3,2,1,0:T(8,128)}, u32[]{:S(2)}) copy-start(f32[1,16,128,128]{3,2,1,0:T(8,128)} %cond_ref.1) | copy-start | bytes 3145732
  3.1 1.2 %copy-start.2 = (f32[1,16,128,128]{3,2,1,0:T(8,128)S(1)}, f32[1,16,128,128]{3,2,1,0:T(8,128)}, u32[]{:S(2)}) copy-start(f32[1,16,128,128]{3,2,1,0:T(8,128)} %heat_ref.1) | copy-start | bytes 3145732
  4.3 0.8 %copy-start.3 = (f32[1,128,128]{2,1,0:T(8,128)S(1)}, f32[1,128,128]{2,1,0:T(8,128)}, u32[]{:S(2)}) copy-start(f32[1,128,128]{2,1,0:T(8,128)} %wall_ref.1) | copy-start | bytes 196612
  5.1 0.7 copy-start.4
  5.8 0.7 copy-start.5
  6.5 0.7 copy-start.6
where the time goes:
time: 83.1 us; the launch traced here: 82.9 us
  Pallas kernels  74.1 us (89%)
  local copies, waits for them, and re-layouts  8.07 us (10%)
    pallas_call x1, Pallas kernels, part(): pl.pallas_call(functools.partial(kernel, n), out_shape=(jax.ShapeDtypeStr...  74.1 us
    unnamed x16, local copies, waits for them, and re-layouts  8.07 us

commit v1 on v0

v1 whole, which is shorter than its diff:
```python
import functools

import jax
import jax.numpy as jnp
from jax import lax
from jax.experimental import pallas as pl
from jax.experimental.pallas import tpu as pltpu
from jax.sharding import PartitionSpec as P

MESH = pl.DeviceIdType.MESH
ITERS, SWEEPS = 2, 3
CY, CX, LZ = 16, 128, 128
TILES = CX // 8 + 1
ROWS = 8 * TILES
PAD = ROWS + 16
F32 = jnp.float32
AW, AE, AS, AN, AB, AA, AD, SRC = range(8)


def tile(i, shift=0):
    return pl.ds(8 + 8 * i + shift, 8)


def row8(i):
    return pl.ds(8 * i, 8)


def remote(src, dst, send, recv, device):
    return pltpu.make_async_remote_copy(
        src_ref=src, dst_ref=dst, send_sem=send, recv_sem=recv, device_id=device, device_id_type=MESH
    )


def split3(x):
    hi = x.astype(jnp.bfloat16)
    rest = x - hi.astype(F32)
    mid = rest.astype(jnp.bfloat16)
    low = (rest - mid.astype(F32)).astype(jnp.bfloat16)
    return hi, mid, low


def pick(chooser, x):
    return sum(jnp.dot(chooser, part, preferred_element_type=F32) for part in split3(x))


def kernel(
    n, theta_ref, cond_ref, vel_ref, heat_ref, wall_ref, kind_ref, block_ref, row_ref,
    theta_out, wall_out,
    th, kb, vb, hb, co, st, sk, sv, sco, sw, pz,
    xs, xr, qo, qs, qr, cr, qt, qtr, ct, wx, wp, wc, tr,
    sb, rb, choose_send, choose_recv, kinds, blocks, rows,
    load_sem, send_sem, recv_sem, wall_send, wall_recv, theta_send, theta_recv, many_send, many_recv,
):
    b, s = lax.axis_index("blk"), lax.axis_index("span")
    chunk = 2 * CX // n
    east, west = lax.rem(b + 1, n), lax.rem(b + n - 1, n)
    E, W, Z, ZE, ZW = (east, s), (west, s), (b, 1 - s), (east, 1 - s), (west, 1 - s)
    own, planes = pl.ds(8, CX), pl.ds(1, CY)

    loads = [
        pltpu.make_async_copy(kind_ref, kinds, load_sem.at[5]),
        pltpu.make_async_copy(block_ref, blocks, load_sem.at[6]),
        pltpu.make_async_copy(row_ref, rows, load_sem.at[7]),
        pltpu.make_async_copy(theta_ref.at[0], th.at[0, planes, own], load_sem.at[0]),
        pltpu.make_async_copy(cond_ref.at[0], kb.at[:, own], load_sem.at[1]),
        pltpu.make_async_copy(vel_ref.at[0], vb.at[:, :, pl.ds(0, CX)], load_sem.at[2]),
        pltpu.make_async_copy(heat_ref.at[0], hb.at[:, pl.ds(0, CX)], load_sem.at[3]),
        pltpu.make_async_copy(wall_ref.at[0], th.at[0, 0, own], load_sem.at[4]),
    ]
    for load in loads:
        load.start()

    rb[:, pl.ds(b, 1)] = jnp.zeros((2, 1, chunk, LZ), F32)

    barrier = pltpu.get_barrier_semaphore()

    def greet(d, carry):
        pl.semaphore_signal(barrier, inc=1, device_id=(lax.rem(b + d, n), s), device_id_type=MESH)
        return carry

    lax.fori_loop(1, n, greet, 0)
    for peer in (Z, ZE, ZW):
        pl.semaphore_signal(barrier, inc=1, device_id=peer, device_id_type=MESH)

    lane = lax.broadcasted_iota(jnp.int32, (8, LZ), 1)
    sub = lax.broadcasted_iota(jnp.int32, (8, LZ), 0)
    group, place = lane // 8, lane % 8
    first_lane, last_lane = lane == 0, lane == LZ - 1
    low_half = place < 4
    middle = (place >= 2) & (place < 6)
    near = sub < 4
    last = TILES - 1

    for t in range(4):
        th[t, CY + 1] = jnp.zeros((PAD, LZ), F32)

    for load in loads:
        load.wait()
    fluid = kinds[b].astype(F32)
    metal = 1.0 - fluid
    same_west = 1.0 - jnp.abs(kinds[west].astype(F32) - fluid)
    same_east = 1.0 - jnp.abs(kinds[east].astype(F32) - fluid)

    def edges(load):
        out = pltpu.roll(load(0), 4, 1)
        for y in range(1, CY):
            out = jnp.where(group == y, pltpu.roll(load(y), (8 * y + 4) % LZ, 1), out)
        return out

    def pack_static(at, at_pad):
        q_k = edges(lambda y: kb[y, at_pad])
        q_v = [edges(lambda y, d=d: vb[d, y, at]) for d in range(3)]
        q_h = edges(lambda y: hb[y, at])
        return [q_k] + q_v + [q_h]

    def paired(q):
        return [
            q[0],
            jnp.where(middle, q[1], pltpu.roll(q[2], 4, 1)),
            jnp.where(middle, q[3], pltpu.roll(q[4], 4, 1)),
        ]

    def pack_tile(i, carry):
        at = pl.ds(pl.multiple_of(8 * i, 8), 8)
        at_pad = pl.ds(pl.multiple_of(8 * i + 8, 8), 8)
        q_th, q_static = edges(lambda y: th[0, y + 1, at_pad]), pack_static(at, at_pad)
        qt[0, at] = q_th
        for slot, q in enumerate(q_static):
            qo[slot, at] = q
        for slot, q in enumerate(paired(q_static)):
            qs[slot, at] = q
        return carry

    lax.fori_loop(0, TILES - 1, pack_tile, 0, unroll=2)

    def pack_rows(y, carry):
        end, pad_end = pl.ds(CX - 8, 8), pl.ds(CX, 8)
        xs[0, 0, y] = jnp.where(sub >= 5, th[0, y + 1, pad_end], pltpu.roll(kb[y, pad_end], 5, 0))
        xs[0, 1, y] = jnp.where(
            sub >= 6,
            vb[0, y, end],
            jnp.where(
                sub >= 4,
                pltpu.roll(vb[1, y, end], 6, 0),
                jnp.where(sub >= 2, pltpu.roll(vb[2, y, end], 4, 0), pltpu.roll(hb[y, end], 2, 0)),
            ),
        )
        zero, pad_zero = pl.ds(0, 8), pl.ds(8, 8)
        xs[1, 0, y] = jnp.where(sub < 3, th[0, y + 1, pad_zero], pltpu.roll(kb[y, pad_zero], 3, 0))
        xs[1, 1, y] = jnp.where(
            sub < 2,
            vb[0, y, zero],
            jnp.where(
                sub < 4,
                pltpu.roll(vb[1, y, zero], 2, 0),
                jnp.where(sub < 6, pltpu.roll(vb[2, y, zero], 4, 0), pltpu.roll(hb[y, zero], 6, 0)),
            ),
        )
        return carry

    lax.fori_loop(0, CY, pack_rows, 0, unroll=4)

    pl.semaphore_wait(barrier, n + 2)

    def wall_copies(r, t):
        plane, ss, rs = th.at[t, 0], wall_send.at[r], wall_recv.at[r]
        tail, head = plane.at[pl.ds(CX, 8)], plane.at[pl.ds(8, 8)]
        return [
            remote(tail, wx.at[r, 0], ss.at[0], rs.at[0], E),
            remote(head, wx.at[r, 1], ss.at[1], rs.at[1], W),
            remote(tail, wc.at[r, 0], ss.at[3], rs.at[3], ZE),
            remote(head, wc.at[r, 1], ss.at[4], rs.at[4], ZW),
            remote(plane.at[own], wp.at[r], ss.at[2], rs.at[2], Z),
        ]

    def theta_strip_copies(r):
        q, ss, rs = qt.at[r], theta_send.at[r], theta_recv.at[r]
        return [
            remote(q.at[pl.ds(CX - 8, 8)], ct.at[r, 0], ss.at[1], rs.at[1], ZE),
            remote(q.at[pl.ds(0, 8)], ct.at[r, 1], ss.at[2], rs.at[2], ZW),
            remote(q, qtr.at[r], ss.at[0], rs.at[0], Z),
        ]

    theta_copies = [
        remote(th.at[3, planes, pl.ds(CX, 8)], tr.at[0], theta_send.at[1, 3], theta_recv.at[1, 3], E),
        remote(th.at[3, planes, pl.ds(8, 8)], tr.at[1], theta_send.at[1, 4], theta_recv.at[1, 4], W),
    ]
    static_copies = [
        remote(xs.at[0], xr.at[0], send_sem.at[0], recv_sem.at[0], E),
        remote(xs.at[1], xr.at[1], send_sem.at[1], recv_sem.at[1], W),
        remote(qs.at[:, pl.ds(CX - 8, 8)], cr.at[0], send_sem.at[3], recv_sem.at[3], ZE),
        remote(qs.at[:, pl.ds(0, 8)], cr.at[1], send_sem.at[4], recv_sem.at[4], ZW),
        remote(qs, qr, send_sem.at[2], recv_sem.at[2], Z),
    ]
    for copy in static_copies + theta_strip_copies(0) + wall_copies(0, 0):
        copy.start()

    mine = jnp.broadcast_to(blocks[...].astype(F32), (CX, CX))
    theirs = jnp.broadcast_to(rows[...].astype(F32), (CX, CX))
    mine_t, theirs_t = mine.T, theirs.T
    at_row = lax.broadcasted_iota(jnp.int32, (CX, CX), 0)
    at_col = lax.broadcasted_iota(jnp.int32, (CX, CX), 1)
    alike = mine_t == mine
    rank = jnp.sum(jnp.where(alike & (at_row < at_col), 1.0, 0.0), axis=0, keepdims=True)
    code = (chunk * mine[0:1] + rank).astype(jnp.int32)
    choose_send[...] = jnp.where(
        lax.broadcasted_iota(jnp.int32, (2 * CX, CX), 0) == code, 1.0, 0.0
    ).astype(jnp.bfloat16)
    rank_t = jnp.sum(jnp.where(alike & (theirs < theirs_t), 1.0, 0.0), axis=1, keepdims=True)
    code_t = (chunk * mine_t[:, 0:1] + rank_t).astype(jnp.int32)
    choose_recv[...] = jnp.where(
        lax.broadcasted_iota(jnp.int32, (CX, 2 * CX), 1) == code_t, 1.0, 0.0
    ).astype(jnp.bfloat16)

    for copy in static_copies:
        copy.wait()

    rows_last = row8(last)

    def unpack_rows(y, carry):
        e0, e1, w0, w1 = xr[1, 0, y], xr[1, 1, y], xr[0, 0, y], xr[0, 1, y]
        t = jnp.where(near, e0, w0)
        th[0, y + 1, tile(last)] = t
        th[0, y + 1, tile(-1)] = t
        th[0, y + 1, tile(TILES)] = th[0, y + 1, tile(0)]
        k = jnp.where(near, pltpu.roll(e0, 5, 0), pltpu.roll(w0, 3, 0))
        kb[y, tile(last)] = k
        kb[y, tile(-1)] = k
        kb[y, tile(TILES)] = kb[y, tile(0)]
        vb[0, y, rows_last] = jnp.where(near, e1, w1)
        vb[1, y, rows_last] = jnp.where(near, pltpu.roll(e1, 6, 0), pltpu.roll(w1, 2, 0))
        vb[2, y, rows_last] = jnp.where(near, pltpu.roll(e1, 4, 0), pltpu.roll(w1, 4, 0))
        hb[y, rows_last] = jnp.where(near, pltpu.roll(e1, 2, 0), pltpu.roll(w1, 6, 0))
        return carry

    lax.fori_loop(0, CY, unpack_rows, 0, unroll=4)

    def put_strip(ref, at, own_q, other_q):
        ref[0, at] = jnp.where(low_half, other_q, own_q)
        ref[1, at] = jnp.where(low_half, own_q, other_q)

    def put_static(at, at_pad, own_q, other_q):
        put_strip(sk, at_pad, own_q[0], other_q[0])
        for slot in range(2):
            t = other_q[1 + slot]
            put_strip(sv.at[2 * slot], at, own_q[1 + 2 * slot], t)
            put_strip(sv.at[2 * slot + 1], at, own_q[2 + 2 * slot], pltpu.roll(t, LZ - 4, 1))

    def static_strip(i, carry):
        at = pl.ds(pl.multiple_of(8 * i, 8), 8)
        at_pad = pl.ds(pl.multiple_of(8 * i + 8, 8), 8)
        put_static(at, at_pad, [qo[slot, at] for slot in range(5)], [qr[slot, at] for slot in range(3)])
        return carry

    lax.fori_loop(0, TILES - 1, static_strip, 0, unroll=4)
    put_static(
        rows_last, tile(last), pack_static(rows_last, tile(last)),
        [jnp.where(near, cr[1, slot], cr[0, slot]) for slot in range(3)],
    )

    def wrap(ref):
        for side in range(2):
            ref[side, tile(-1)] = ref[side, tile(last)]
            ref[side, tile(TILES)] = ref[side, tile(0)]

    wrap(sk)

    def coefficients(k, k_w, k_e, k_s, k_n, k_b, k_a, v, mask_w, mask_e, bottom, top):
        v = [fluid * x for x in v]
        a_w = mask_w(0.5 * (k + k_w) + jnp.maximum(v[0], 0.0))
        a_e = mask_e(0.5 * (k + k_e) - jnp.minimum(v[0], 0.0))
        a_b = 0.5 * (k + k_b) + jnp.maximum(v[1], 0.0)
        a_b = a_b * (1.0 - metal * bottom)
        a_a = (0.5 * (k + k_a) - jnp.minimum(v[1], 0.0)) * (1.0 - top)
        a_s = 0.5 * (k + k_s) + jnp.maximum(v[2], 0.0)
        a_n = 0.5 * (k + k_n) - jnp.minimum(v[2], 0.0)
        a_d = 1.0 - (a_w + a_e + a_s + a_n + a_b + a_a)
        return a_w, a_e, a_s, a_n, a_b + metal * bottom, a_a, a_d

    whole, whole_w, whole_e = pl.ds(8, ROWS), pl.ds(7, ROWS), pl.ds(9, ROWS)
    strip_row = lax.broadcasted_iota(jnp.int32, (ROWS, LZ), 0)
    strip_group = lax.broadcasted_iota(jnp.int32, (ROWS, LZ), 1) // 8
    strip_first = strip_group == 0

    def strip_coefficients(side, carry):
        k = sk[side, whole]
        a = coefficients(
            k, sk[side, whole_w], sk[side, whole_e], pltpu.roll(k, 1, 1), pltpu.roll(k, LZ - 1, 1),
            jnp.where(strip_first, k, pltpu.roll(k, 8, 1)), pltpu.roll(k, LZ - 8, 1), [sv[d, side] for d in range(3)],
            lambda x: jnp.where(strip_row == 0, same_west * x, x),
            lambda x: jnp.where(strip_row == CX - 1, same_east * x, x),
            strip_first.astype(F32), (strip_group == CY - 1).astype(F32),
        )
        for slot, value in enumerate(a):
            sco[slot, side] = value
        return carry

    lax.fori_loop(0, 2, strip_coefficients, 0)
    def plane_coefficients(y, carry):
        bottom = (y == 0).astype(F32)
        top = (y == CY - 1).astype(F32)
        below, above = jnp.maximum(y - 1, 0), jnp.minimum(y + 1, CY - 1)
        for i in range(TILES):
            k = kb[y, tile(i)]
            k_s, k_n = pltpu.roll(k, 1, 1), pltpu.roll(k, LZ - 1, 1)
            mask_w = (lambda x: jnp.where(sub == 0, same_west * x, x)) if i == 0 else (lambda x: x)
            mask_e = (lambda x: jnp.where(sub == 7, same_east * x, x)) if i == last - 1 else (lambda x: x)
            a = coefficients(
                k, kb[y, tile(i, -1)], kb[y, tile(i, 1)], k_s, k_n, kb[below, tile(i)], kb[above, tile(i)],
                [vb[d, y, row8(i)] for d in range(3)], mask_w, mask_e, bottom, top,
            )
            for slot, value in enumerate(a):
                co[slot, y, row8(i)] = value
        return carry

    edge_two, edge_one = (lane < 2) | (lane >= LZ - 2), first_lane | last_lane

    def sweep(t, following, step, first, end):
        def pair(g, carry):
            for half in range(2):
                y = 2 * g + half
                for i in range(TILES):
                    at = row8(i)
                    c = th[t, y + 1, tile(i)]
                    new = (
                        (hb[y, at] + co[AD, y, at] * c)
                        + (co[AW, y, at] * th[t, y + 1, tile(i, -1)] + co[AE, y, at] * th[t, y + 1, tile(i, 1)])
                        + (co[AS, y, at] * pltpu.roll(c, 1, 1) + co[AN, y, at] * pltpu.roll(c, LZ - 1, 1))
                        + (co[AB, y, at] * th[t, y, tile(i)] + co[AA, y, at] * th[t, y + 2, tile(i)])
                    )
                    if step > 0:
                        new = jnp.where(edge_two if step == 1 else edge_one, pz[step - 1, y, at], new)
                    th[following, y + 1, tile(i)] = new
                    if i == last:
                        th[following, y + 1, tile(-1)] = new
                    if i == 0:
                        th[following, y + 1, tile(TILES)] = new
            return carry

        lax.fori_loop(first, end, pair, 0)

    def strip_sweep(m, carry):
        step, side = m // 2, m % 2
        c = st[step, side, whole]
        below = jnp.where(strip_first, sw[side], pltpu.roll(c, 8, 1))
        new = (
            (sv[3, side] + sco[AD, side] * c)
            + (sco[AW, side] * st[step, side, whole_w] + sco[AE, side] * st[step, side, whole_e])
            + (sco[AS, side] * pltpu.roll(c, 1, 1) + sco[AN, side] * pltpu.roll(c, LZ - 1, 1))
            + (sco[AB, side] * below + sco[AA, side] * pltpu.roll(c, LZ - 8, 1))
        )
        st[step + 1, side, whole] = new
        st[step + 1, side, tile(-1)] = new[ROWS - 8 :]
        st[step + 1, side, tile(TILES)] = new[:8]
        return carry

    def spread(slot, first, end):
        strips = [jnp.where(low_half, st[slot + 2, 1, tile(i)], st[slot + 2, 0, tile(i)]) for i in range(TILES)]
        for y in range(first, end):
            for i in range(TILES):
                pz[slot, y, row8(i)] = pltpu.roll(strips[i], 124 - 8 * y, 1)

    def send_faces(r, t):
        field, wall = th[t, 1, own], th[t, 0, own]
        sent = fluid * (kb[0, own] * (field - wall)) + metal * field
        sb[...] = pick(choose_send[...], sent).reshape(n, chunk, LZ)

        def to(zd, i):
            x, y, c = (b // 4) % 4 + 3 - i // 4, (b // 2) % 2 + 1 - (i // 2) % 2, b % 2 + 1 - i % 2
            z = lax.rem(b // 16 + zd, n // 16)
            t = z * 16 + lax.rem(x, 4) * 4 + lax.rem(y, 2) * 2 + lax.rem(c, 2)
            remote(sb.at[t], rb.at[r, b], many_send.at[r], many_recv.at[r], (t, s)).start()

        for zd in (4, 3, 5, 2, 6, 1, 7):
            if zd < n // 16:
                lax.fori_loop(0, 16, lambda i, carry, zd=zd: (to(zd, i), carry)[1], 0, unroll=2)
        lax.fori_loop(0, 15, lambda i, carry: (to(0, i), carry)[1], 0, unroll=3)

    def receive_faces(r):
        others = pl.ds(0, n - 1)
        remote(sb.at[others], rb.at[r, others], many_send.at[r], many_recv.at[r], Z).wait()
        return pick(choose_recv[...], rb[r].reshape(2 * CX, LZ))

    def theta_strip(r):
        def one(i, carry):
            at = pl.ds(pl.multiple_of(8 * i, 8), 8)
            at_pad = pl.ds(pl.multiple_of(8 * i + 8, 8), 8)
            put_strip(st.at[0], at_pad, qt[r, at], qtr[r, at])
            own_w = pltpu.roll(th[3 * r, 0, at_pad], 4, 1)
            put_strip(sw, at, own_w, pltpu.roll(wp[r, at], 4, 1))
            return carry

        lax.fori_loop(0, TILES - 1, one, 0, unroll=4)
        put_strip(
            st.at[0], tile(last), edges(lambda y: th[3 * r, y + 1, tile(last)]), jnp.where(near, ct[r, 1], ct[r, 0])
        )
        wrap(st.at[0])
        wall_last = jnp.where(near, wx[r, 1], wx[r, 0])
        th[3 * r, 0, tile(last)] = wall_last
        put_strip(
            sw, rows_last, pltpu.roll(wall_last, 4, 1), pltpu.roll(jnp.where(near, wc[r, 1], wc[r, 0]), 4, 1)
        )
        wall = th[3 * r, 0, whole]
        for t in range(4):
            th[t, 0, whole] = wall

    def unpack_theta(y, carry):
        t = jnp.where(near, tr[1, y], tr[0, y])
        th[3, y + 1, tile(last)] = t
        th[3, y + 1, tile(-1)] = t
        return carry

    def pack_theta(i, carry):
        at_pad = pl.ds(pl.multiple_of(8 * i + 8, 8), 8)
        qt[1, pl.ds(pl.multiple_of(8 * i, 8), 8)] = edges(lambda y: th[3, y + 1, at_pad])
        return carry

    store = pltpu.make_async_copy(th.at[2, planes, own], theta_out.at[0], load_sem.at[0])

    def iteration(r):
        for copy in theta_strip_copies(r) + wall_copies(r, 3 * r):
            copy.wait()
        if r == 1:
            for copy in theta_copies:
                copy.wait()
            lax.fori_loop(0, CY, unpack_theta, 0, unroll=4)
        theta_strip(r)
        lax.fori_loop(0, 2 * SWEEPS, strip_sweep, 0)

        def phase(late, carry):
            for slot in range(2):

                @pl.when(late == 0)
                def _():
                    spread(slot, 0, 4)

                @pl.when(late == 1)
                def _():
                    spread(slot, 4, CY)

            if r == 0:
                lax.fori_loop(4 * late, 4 + (CY - 4) * late, plane_coefficients, 0)
            for step in range(SWEEPS):
                sweep(
                    (3 * r + step) % 4, (3 * r + step + 1) % 4, step,
                    late * (2 - step), (1 - late) * max(2 - step, 1) + late * (CY // 2),
                )

            @pl.when(late == 0)
            def _():
                send_faces(r, (3 * r + 3) % 4)

            return carry

        lax.fori_loop(0, 2, phase, 0)
        if r == 0:
            lax.fori_loop(0, TILES - 1, pack_theta, 0, unroll=4)
            for copy in theta_copies + theta_strip_copies(1):
                copy.start()
        else:
            store.start()
        th[3 - r, 0, own] = receive_faces(r)
        if r == 0:
            for copy in wall_copies(1, 3):
                copy.start()

    for r in range(ITERS):
        iteration(r)
    wall_out[0] = th[2, 0, own]
    store.wait()


def solution(mesh):
    n = mesh.shape["blk"]
    chunk = 2 * CX // n

    def part(theta, cond, vel, heat, wall, kinds, blocks, rows):
        hbm = pl.BlockSpec(memory_space=pltpu.HBM)
        anywhere = pl.BlockSpec(memory_space=pl.ANY)
        vmem = pl.BlockSpec(memory_space=pltpu.VMEM)
        buf = lambda *shape: pltpu.VMEM(shape, F32)
        return pl.pallas_call(
            functools.partial(kernel, n),
            out_shape=(
                jax.ShapeDtypeStruct(theta.shape, F32),
                jax.ShapeDtypeStruct(wall.shape, F32),
            ),
            in_specs=[hbm] * 8,
            out_specs=(anywhere, vmem),
            scratch_shapes=[
                buf(4, CY + 2, PAD, LZ),
                buf(CY, PAD, LZ),
                buf(3, CY, ROWS, LZ),
                buf(CY, ROWS, LZ),
                buf(7, CY, ROWS, LZ),
                buf(4, 2, PAD, LZ),
                buf(2, PAD, LZ),
                buf(4, 2, ROWS, LZ),
                buf(7, 2, ROWS, LZ),
                buf(2, ROWS, LZ),
                buf(2, CY, ROWS, LZ),
                buf(2, 2, CY, 8, LZ),
                buf(2, 2, CY, 8, LZ),
                buf(5, CX, LZ),
                buf(3, CX, LZ),
                buf(3, CX, LZ),
                buf(2, 3, 8, LZ),
                buf(2, CX, LZ),
                buf(2, CX, LZ),
                buf(2, 2, 8, LZ),
                buf(2, 2, 8, LZ),
                buf(2, CX, LZ),
                buf(2, 2, 8, LZ),
                buf(2, CY, 8, LZ),
                buf(n, chunk, LZ),
                buf(2, n, chunk, LZ),
                pltpu.VMEM((2 * CX, CX), jnp.bfloat16),
                pltpu.VMEM((CX, 2 * CX), jnp.bfloat16),
                pltpu.SMEM((n,), jnp.int32),
                pltpu.VMEM((1, CX), jnp.int32),
                pltpu.VMEM((1, CX), jnp.int32),
                pltpu.SemaphoreType.DMA((8,)),
                pltpu.SemaphoreType.DMA((5,)),
                pltpu.SemaphoreType.DMA((5,)),
                pltpu.SemaphoreType.DMA((2, 5)),
                pltpu.SemaphoreType.DMA((2, 5)),
                pltpu.SemaphoreType.DMA((2, 5)),
                pltpu.SemaphoreType.DMA((2, 5)),
                pltpu.SemaphoreType.DMA((2,)),
                pltpu.SemaphoreType.DMA((2,)),
            ],
            compiler_params=pltpu.CompilerParams(
                collective_id=0, has_side_effects=True, vmem_limit_bytes=56 * 2**20
            ),
        )(theta, cond, vel, heat, wall, kinds, blocks, rows)

    whole = P("blk", None, None, "span")
    rows = P("blk", None, "span")
    return jax.shard_map(
        part,
        mesh=mesh,
        in_specs=(whole, whole, P("blk", None, None, None, "span"), whole, rows, P(), P("blk", None), P("blk", None)),
        out_specs=(whole, rows),
        check_vma=False,
    )
```

time: 83.1 us -> 60.8 us (0.73)
  Pallas kernels: 74.1 us -> 56.3 us
  local copies, waits for them, and re-layouts: 8.07 us -> 3.77 us
    pallas_call x1, Pallas kernels: 74.1 us -> 56.3 us  [part(): pl.pallas_call(functools.partial(kernel, n), out_shape=(jax.ShapeDtypeStr...]
    unnamed x16 -> x2, local copies, waits for them, and re-layouts: 8.07 us -> 3.77 us
where the time goes in v1:
time: 60.8 us; the launch traced here: 60.7 us
  Pallas kernels  56.3 us (93%)
  local copies, waits for them, and re-layouts  3.77 us (6%)
  between operations  0.64 us (1%)
    pallas_call x1, Pallas kernels, part(): pl.pallas_call(functools.partial(kernel, n), out_shape=(jax.ShapeDtypeStr...  56.3 us
    unnamed x2, local copies, waits for them, and re-layouts  3.77 us

profile of v1, /device:TPU:1, one launch (start us, length us, event | category | flops | bytes accessed | tf_op | source)
XLA Modules:
  0.0 60.7 jit_solution(10959617655700251812)
XLA Ops:
  0.6 56.3 %shard_map.95 = (f32[1,16,128,128]{3,2,1,0:T(8,128)}, f32[1,128,128]{2,1,0:T(8,128)}) custom-call(f32[1,16,128,128]{3,2,1,0:T(8,128)} %theta_ref.1, f32[1,16,128,128]{3,2,1,0:T(8,128)} %cond_ref.1, f32[1,3,16,128,128]{4,3,2,1,0:T(8,128)} %vel_ref.1, f32[1,16,128,128]{3,2,1,0:T(8,128)} %heat_ref.1, f32[1,128,128]{2,1,0:T(8,128)} %wall_ref.1, s32[128]{0:T(128)} %kind_ref.1, ...), custom_call_target="tpu_custom_call" | custom-call | tf_op jit(solution)/shard_map/pallas_call | solution.py:482
  56.9 2.3 %copy.12 = f32[1,16,128,128]{3,2,1,0:T(8,128)} copy(f32[1,16,128,128]{3,2,1,0:T(8,128)} %get-tuple-element.4) | data formatting | bytes 2097152
  59.2 1.5 %copy.13 = f32[1,128,128]{2,1,0:T(8,128)} copy(f32[1,128,128]{2,1,0:T(8,128)} %get-tuple-element.5) | data formatting | bytes 131072

commit v2 on v1

--- a/solution.py
+++ b/solution.py
@@ -10,6 +10,7 @@
 MESH = pl.DeviceIdType.MESH
 ITERS, SWEEPS = 2, 3
 CY, CX, LZ = 16, 128, 128
+LOW = 4
 TILES = CX // 8 + 1
 ROWS = 8 * TILES
 PAD = ROWS + 16
@@ -47,9 +48,10 @@
     n, theta_ref, cond_ref, vel_ref, heat_ref, wall_ref, kind_ref, block_ref, row_ref,
     theta_out, wall_out,
     th, kb, vb, hb, co, st, sk, sv, sco, sw, pz,
-    xs, xr, qo, qs, qr, cr, qt, qtr, ct, wx, wp, wc, tr,
+    xs, xr, qo, qs, qr, cr, qx, cx, qa, qar, ca, qt, qtr, ct, qw, qwr, wx, wc, tr,
     sb, rb, choose_send, choose_recv, kinds, blocks, rows,
-    load_sem, send_sem, recv_sem, wall_send, wall_recv, theta_send, theta_recv, many_send, many_recv,
+    load_sem, low_send, low_recv, mid_send, mid_recv, rest_send, rest_recv, wall_send, wall_recv, theta_send, theta_recv,
+    many_send, many_recv, known,
 ):
     b, s = lax.axis_index("blk"), lax.axis_index("span")
     chunk = 2 * CX // n
@@ -72,14 +74,14 @@
 
     rb[:, pl.ds(b, 1)] = jnp.zeros((2, 1, chunk, LZ), F32)
 
+    def line(count, stride):
+        at = lax.rem(b // stride, count)
+        return [(b + (lax.rem(at + d, count) - at) * stride, s) for d in range(1, count)]
+
+    line_z, line_x, line_y = line(n // 16, 16), line(4, 4), line(4, 1)
     barrier = pltpu.get_barrier_semaphore()
-
-    def greet(d, carry):
-        pl.semaphore_signal(barrier, inc=1, device_id=(lax.rem(b + d, n), s), device_id_type=MESH)
-        return carry
-
-    lax.fori_loop(1, n, greet, 0)
-    for peer in (Z, ZE, ZW):
+    beside = [E, W, Z, ZE, ZW] + line_z + line_x + line_y
+    for peer in beside:
         pl.semaphore_signal(barrier, inc=1, device_id=peer, device_id_type=MESH)
 
     lane = lax.broadcasted_iota(jnp.int32, (8, LZ), 1)
@@ -101,9 +103,9 @@
     same_west = 1.0 - jnp.abs(kinds[west].astype(F32) - fluid)
     same_east = 1.0 - jnp.abs(kinds[east].astype(F32) - fluid)
 
-    def edges(load):
+    def edges(load, count=CY):
         out = pltpu.roll(load(0), 4, 1)
-        for y in range(1, CY):
+        for y in range(1, count):
             out = jnp.where(group == y, pltpu.roll(load(y), (8 * y + 4) % LZ, 1), out)
         return out
 
@@ -123,12 +125,18 @@
     def pack_tile(i, carry):
         at = pl.ds(pl.multiple_of(8 * i, 8), 8)
         at_pad = pl.ds(pl.multiple_of(8 * i + 8, 8), 8)
-        q_th, q_static = edges(lambda y: th[0, y + 1, at_pad]), pack_static(at, at_pad)
-        qt[0, at] = q_th
-        for slot, q in enumerate(q_static):
-            qo[slot, at] = q
-        for slot, q in enumerate(paired(q_static)):
-            qs[slot, at] = q
+        q = pack_static(at, at_pad) + [edges(lambda y: th[0, y + 1, at_pad])]
+        sent = [q[5]] + paired(q)
+        for slot in range(6):
+            qo[slot, at] = q[slot]
+        for slot in range(2):
+            qs[slot, at] = jnp.where(group < 8, pltpu.roll(sent[2 * slot], 64, 1), sent[2 * slot + 1])
+        for half in range(2):
+            parts = [pltpu.roll(q, (32 * (slot - half)) % LZ, 1) if slot != half else q for slot, q in enumerate(sent)]
+            out = parts[0]
+            for slot in range(1, 4):
+                out = jnp.where(group >= 4 * slot, parts[slot], out)
+            qa[half, at] = out
         return carry
 
     lax.fori_loop(0, TILES - 1, pack_tile, 0, unroll=2)
@@ -160,39 +168,62 @@
 
     lax.fori_loop(0, CY, pack_rows, 0, unroll=4)
 
-    pl.semaphore_wait(barrier, n + 2)
+    def pack_wall(r, t):
+        out = pltpu.roll(th[t, 0, tile(0)], 4, 1)
+        for i in range(1, TILES - 1):
+            out = jnp.where(group == i, pltpu.roll(th[t, 0, tile(i)], (8 * i + 4) % LZ, 1), out)
+        qw[r] = out
+
+    pack_wall(0, 0)
+
+    pl.semaphore_wait(barrier, len(beside))
+    for peer in line_x:
+        pl.semaphore_signal(known.at[0], inc=1, device_id=peer, device_id_type=MESH)
 
     def wall_copies(r, t):
         plane, ss, rs = th.at[t, 0], wall_send.at[r], wall_recv.at[r]
         tail, head = plane.at[pl.ds(CX, 8)], plane.at[pl.ds(8, 8)]
         return [
+            remote(tail, wc.at[r, 0], ss.at[3], rs.at[3], ZE),
+            remote(head, wc.at[r, 1], ss.at[4], rs.at[4], ZW),
             remote(tail, wx.at[r, 0], ss.at[0], rs.at[0], E),
             remote(head, wx.at[r, 1], ss.at[1], rs.at[1], W),
-            remote(tail, wc.at[r, 0], ss.at[3], rs.at[3], ZE),
-            remote(head, wc.at[r, 1], ss.at[4], rs.at[4], ZW),
-            remote(plane.at[own], wp.at[r], ss.at[2], rs.at[2], Z),
+            remote(qw.at[r], qwr.at[r], ss.at[2], rs.at[2], Z),
         ]
 
-    def theta_strip_copies(r):
-        q, ss, rs = qt.at[r], theta_send.at[r], theta_recv.at[r]
+    head, tail = pl.ds(0, 8), pl.ds(CX - 8, 8)
+    low, mid, rest = pl.ds(0, LOW), pl.ds(LOW, LOW), pl.ds(2 * LOW, CY - 2 * LOW)
+
+    def theta_copies(late):
+        ss, rs = theta_send.at[late], theta_recv.at[late]
+        at, to = (pl.ds(1 + LOW, CY - LOW), pl.ds(LOW, CY - LOW)) if late else (pl.ds(1, LOW), low)
         return [
-            remote(q.at[pl.ds(CX - 8, 8)], ct.at[r, 0], ss.at[1], rs.at[1], ZE),
-            remote(q.at[pl.ds(0, 8)], ct.at[r, 1], ss.at[2], rs.at[2], ZW),
-            remote(q, qtr.at[r], ss.at[0], rs.at[0], Z),
+            remote(qt.at[late, tail], ct.at[late, 0], ss.at[1], rs.at[1], ZE),
+            remote(qt.at[late, head], ct.at[late, 1], ss.at[2], rs.at[2], ZW),
+            remote(th.at[3, at, pl.ds(CX, 8)], tr.at[0, to], ss.at[3], rs.at[3], E),
+            remote(th.at[3, at, pl.ds(8, 8)], tr.at[1, to], ss.at[4], rs.at[4], W),
+            remote(qt.at[late], qtr.at[late], ss.at[0], rs.at[0], Z),
         ]
 
-    theta_copies = [
-        remote(th.at[3, planes, pl.ds(CX, 8)], tr.at[0], theta_send.at[1, 3], theta_recv.at[1, 3], E),
-        remote(th.at[3, planes, pl.ds(8, 8)], tr.at[1], theta_send.at[1, 4], theta_recv.at[1, 4], W),
+    def part_copies(half, planes, ss, rs):
+        return [
+            remote(qa.at[half, tail], ca.at[half, 0], ss.at[3], rs.at[3], ZE),
+            remote(qa.at[half, head], ca.at[half, 1], ss.at[4], rs.at[4], ZW),
+            remote(xs.at[0, :, planes], xr.at[0, :, planes], ss.at[0], rs.at[0], E),
+            remote(xs.at[1, :, planes], xr.at[1, :, planes], ss.at[1], rs.at[1], W),
+            remote(qa.at[half], qar.at[half], ss.at[2], rs.at[2], Z),
+        ]
+
+    low_copies = part_copies(0, low, low_send, low_recv)
+    mid_copies = part_copies(1, mid, mid_send, mid_recv)
+    rest_copies = [
+        remote(qs.at[:, tail], cr.at[0], rest_send.at[3], rest_recv.at[3], ZE),
+        remote(qs.at[:, head], cr.at[1], rest_send.at[4], rest_recv.at[4], ZW),
+        remote(xs.at[0, :, rest], xr.at[0, :, rest], rest_send.at[0], rest_recv.at[0], E),
+        remote(xs.at[1, :, rest], xr.at[1, :, rest], rest_send.at[1], rest_recv.at[1], W),
+        remote(qs, qr, rest_send.at[2], rest_recv.at[2], Z),
     ]
-    static_copies = [
-        remote(xs.at[0], xr.at[0], send_sem.at[0], recv_sem.at[0], E),
-        remote(xs.at[1], xr.at[1], send_sem.at[1], recv_sem.at[1], W),
-        remote(qs.at[:, pl.ds(CX - 8, 8)], cr.at[0], send_sem.at[3], recv_sem.at[3], ZE),
-        remote(qs.at[:, pl.ds(0, 8)], cr.at[1], send_sem.at[4], recv_sem.at[4], ZW),
-        remote(qs, qr, send_sem.at[2], recv_sem.at[2], Z),
-    ]
-    for copy in static_copies + theta_strip_copies(0) + wall_copies(0, 0):
+    for copy in low_copies + wall_copies(0, 0):
         copy.start()
 
     mine = jnp.broadcast_to(blocks[...].astype(F32), (CX, CX))
@@ -212,8 +243,13 @@
         lax.broadcasted_iota(jnp.int32, (CX, 2 * CX), 1) == code_t, 1.0, 0.0
     ).astype(jnp.bfloat16)
 
-    for copy in static_copies:
+    for copy in mid_copies + rest_copies:
+        copy.start()
+    for copy in low_copies:
         copy.wait()
+    pl.semaphore_wait(known.at[0], len(line_x))
+    for peer in line_y:
+        pl.semaphore_signal(known.at[1], inc=1, device_id=peer, device_id_type=MESH)
 
     rows_last = row8(last)
 
@@ -233,8 +269,6 @@
         hb[y, rows_last] = jnp.where(near, pltpu.roll(e1, 2, 0), pltpu.roll(w1, 6, 0))
         return carry
 
-    lax.fori_loop(0, CY, unpack_rows, 0, unroll=4)
-
     def put_strip(ref, at, own_q, other_q):
         ref[0, at] = jnp.where(low_half, other_q, own_q)
         ref[1, at] = jnp.where(low_half, own_q, other_q)
@@ -246,24 +280,63 @@
             put_strip(sv.at[2 * slot], at, own_q[1 + 2 * slot], t)
             put_strip(sv.at[2 * slot + 1], at, own_q[2 + 2 * slot], pltpu.roll(t, LZ - 4, 1))
 
-    def static_strip(i, carry):
-        at = pl.ds(pl.multiple_of(8 * i, 8), 8)
-        at_pad = pl.ds(pl.multiple_of(8 * i + 8, 8), 8)
-        put_static(at, at_pad, [qo[slot, at] for slot in range(5)], [qr[slot, at] for slot in range(3)])
-        return carry
-
-    lax.fori_loop(0, TILES - 1, static_strip, 0, unroll=4)
-    put_static(
-        rows_last, tile(last), pack_static(rows_last, tile(last)),
-        [jnp.where(near, cr[1, slot], cr[0, slot]) for slot in range(3)],
-    )
+    def split(half, value, before):
+        parts = [pltpu.roll(value, (32 * (half - slot)) % LZ, 1) if slot != half else value for slot in range(4)]
+        return [jnp.where(group < LOW, x, y) for x, y in zip(before, parts)] if half else parts
+
+    def split_strips(half):
+        def one(i, carry):
+            at = pl.ds(pl.multiple_of(8 * i, 8), 8)
+            before = [qx[0, slot, at] for slot in range(4)] if half else None
+            for slot, value in enumerate(split(half, qar[half, at], before)):
+                qx[half, slot, at] = value
+            return carry
+
+        lax.fori_loop(0, TILES - 1, one, 0, unroll=4)
+        for side in range(2):
+            before = [cx[0, side, slot] for slot in range(4)] if half else None
+            for slot, value in enumerate(split(half, ca[half, side], before)):
+                cx[half, side, slot] = value
+
+    def join_rest(value, before):
+        return [
+            jnp.where(group < 8, x, pltpu.roll(value[slot // 2], 64, 1) if slot % 2 == 0 else value[slot // 2])
+            for slot, x in enumerate(before)
+        ]
+
+    def join_strips():
+        def one(i, carry):
+            at = pl.ds(pl.multiple_of(8 * i, 8), 8)
+            all_planes = join_rest([qr[slot, at] for slot in range(2)], [qx[1, slot, at] for slot in range(4)])
+            for slot, value in enumerate(all_planes):
+                qx[2, slot, at] = value
+            return carry
+
+        lax.fori_loop(0, TILES - 1, one, 0, unroll=4)
+        for side in range(2):
+            all_planes = join_rest([cr[side, slot] for slot in range(2)], [cx[1, side, slot] for slot in range(4)])
+            for slot, value in enumerate(all_planes):
+                cx[2, side, slot] = value
+
+    def static_strips(late):
+        def one(i, carry):
+            at = pl.ds(pl.multiple_of(8 * i, 8), 8)
+            at_pad = pl.ds(pl.multiple_of(8 * i + 8, 8), 8)
+            put_strip(st.at[0], at_pad, qo[5, at], qx[late, 0, at])
+            put_static(at, at_pad, [qo[slot, at] for slot in range(5)], [qx[late, slot, at] for slot in range(1, 4)])
+            return carry
+
+        lax.fori_loop(0, TILES - 1, one, 0, unroll=4)
+        other = [jnp.where(near, cx[late, 1, slot], cx[late, 0, slot]) for slot in range(4)]
+        put_strip(st.at[0], tile(last), edges(lambda y: th[0, y + 1, tile(last)]), other[0])
+        put_static(rows_last, tile(last), pack_static(rows_last, tile(last)), other[1:])
+        wrap(st.at[0])
+        wrap(sk)
 
     def wrap(ref):
         for side in range(2):
             ref[side, tile(-1)] = ref[side, tile(last)]
             ref[side, tile(TILES)] = ref[side, tile(0)]
-
-    wrap(sk)
 
     def coefficients(k, k_w, k_e, k_s, k_n, k_b, k_a, v, mask_w, mask_e, bottom, top):
         v = [fluid * x for x in v]
@@ -295,7 +368,6 @@
             sco[slot, side] = value
         return carry
 
-    lax.fori_loop(0, 2, strip_coefficients, 0)
     def plane_coefficients(y, carry):
         bottom = (y == 0).astype(F32)
         top = (y == CY - 1).astype(F32)
@@ -381,28 +453,32 @@
         remote(sb.at[others], rb.at[r, others], many_send.at[r], many_recv.at[r], Z).wait()
         return pick(choose_recv[...], rb[r].reshape(2 * CX, LZ))
 
-    def theta_strip(r):
-        def one(i, carry):
-            at = pl.ds(pl.multiple_of(8 * i, 8), 8)
-            at_pad = pl.ds(pl.multiple_of(8 * i + 8, 8), 8)
-            put_strip(st.at[0], at_pad, qt[r, at], qtr[r, at])
-            own_w = pltpu.roll(th[3 * r, 0, at_pad], 4, 1)
-            put_strip(sw, at, own_w, pltpu.roll(wp[r, at], 4, 1))
-            return carry
-
-        lax.fori_loop(0, TILES - 1, one, 0, unroll=4)
-        put_strip(
-            st.at[0], tile(last), edges(lambda y: th[3 * r, y + 1, tile(last)]), jnp.where(near, ct[r, 1], ct[r, 0])
-        )
-        wrap(st.at[0])
+    def wall_strip(r):
         wall_last = jnp.where(near, wx[r, 1], wx[r, 0])
         th[3 * r, 0, tile(last)] = wall_last
+        wall = th[3 * r, 0, whole]
+        for t in range(4):
+            if t != 3 * r:
+                th[t, 0, whole] = wall
+        q = qwr[r]
+        for i in range(TILES - 1):
+            other = pltpu.roll(q, LZ - 8 * i, 1) if i else q
+            put_strip(sw, row8(i), pltpu.roll(wall[8 * i : 8 * i + 8], 4, 1), other)
         put_strip(
             sw, rows_last, pltpu.roll(wall_last, 4, 1), pltpu.roll(jnp.where(near, wc[r, 1], wc[r, 0]), 4, 1)
         )
-        wall = th[3 * r, 0, whole]
-        for t in range(4):
-            th[t, 0, whole] = wall
+
+    def theta_strips(late):
+        def one(i, carry):
+            at = pl.ds(pl.multiple_of(8 * i, 8), 8)
+            put_strip(st.at[0], pl.ds(pl.multiple_of(8 * i + 8, 8), 8), qt[late, at], qtr[late, at])
+            return carry
+
+        lax.fori_loop(0, TILES - 1, one, 0, unroll=4)
+        put_strip(
+            st.at[0], tile(last), edges(lambda y: th[3, y + 1, tile(last)]), jnp.where(near, ct[late, 1], ct[late, 0])
+        )
+        wrap(st.at[0])
 
     def unpack_theta(y, carry):
         t = jnp.where(near, tr[1, y], tr[0, y])
@@ -410,64 +486,137 @@
         th[3, y + 1, tile(-1)] = t
         return carry
 
-    def pack_theta(i, carry):
-        at_pad = pl.ds(pl.multiple_of(8 * i + 8, 8), 8)
-        qt[1, pl.ds(pl.multiple_of(8 * i, 8), 8)] = edges(lambda y: th[3, y + 1, at_pad])
-        return carry
+    def send_theta(late):
+        def pack(i, carry):
+            at_pad = pl.ds(pl.multiple_of(8 * i + 8, 8), 8)
+            at = pl.ds(pl.multiple_of(8 * i, 8), 8)
+            qt[late, at] = edges(lambda y: th[3, y + 1, at_pad], CY if late else LOW)
+            return carry
+
+        lax.fori_loop(0, TILES - 1, pack, 0, unroll=4)
+        for copy in theta_copies(late):
+            copy.start()
 
     store = pltpu.make_async_copy(th.at[2, planes, own], theta_out.at[0], load_sem.at[0])
 
-    def iteration(r):
-        for copy in theta_strip_copies(r) + wall_copies(r, 3 * r):
-            copy.wait()
-        if r == 1:
-            for copy in theta_copies:
+    def by(p, *values):
+        out = values[0] + p * (values[1] - values[0])
+        if len(values) == 3:
+            out = out + p * (p - 1) // 2 * (values[2] - 2 * values[1] + values[0])
+        return out
+
+    def sweeps(r, p, *bounds):
+        for step in range(SWEEPS):
+            first, end = zip(*[bound[step] for bound in bounds])
+            sweep((3 * r + step) % 4, (3 * r + step + 1) % 4, step, by(p, *first), by(p, *end))
+
+    def when(p, value, action):
+        pl.when(p == value)(action)
+
+    def unpack(take, first, end):
+        lax.fori_loop(first, end, take, 0, unroll=4)
+
+    def spread_both(first, end):
+        for slot in range(2):
+            spread(slot, first, end)
+
+    for copy in wall_copies(0, 0):
+        copy.wait()
+    wall_strip(0)
+
+    def first_iteration(p, carry):
+        @pl.when(p == 0)
+        def _():
+            split_strips(0)
+            unpack(unpack_rows, 0, LOW)
+
+        @pl.when(p == 1)
+        def _():
+            for copy in mid_copies:
                 copy.wait()
-            lax.fori_loop(0, CY, unpack_theta, 0, unroll=4)
-        theta_strip(r)
+            split_strips(1)
+            unpack(unpack_rows, LOW, 2 * LOW)
+
+        @pl.when(p == 2)
+        def _():
+            for copy in rest_copies:
+                copy.wait()
+            join_strips()
+            unpack(unpack_rows, 2 * LOW, CY)
+
+        static_strips(p)
+        lax.fori_loop(0, 2, strip_coefficients, 0)
         lax.fori_loop(0, 2 * SWEEPS, strip_sweep, 0)
-
-        def phase(late, carry):
-            for slot in range(2):
-
-                @pl.when(late == 0)
-                def _():
-                    spread(slot, 0, 4)
-
-                @pl.when(late == 1)
-                def _():
-                    spread(slot, 4, CY)
-
-            if r == 0:
-                lax.fori_loop(4 * late, 4 + (CY - 4) * late, plane_coefficients, 0)
-            for step in range(SWEEPS):
-                sweep(
-                    (3 * r + step) % 4, (3 * r + step + 1) % 4, step,
-                    late * (2 - step), (1 - late) * max(2 - step, 1) + late * (CY // 2),
-                )
-
-            @pl.when(late == 0)
-            def _():
-                send_faces(r, (3 * r + 3) % 4)
-
-            return carry
-
-        lax.fori_loop(0, 2, phase, 0)
-        if r == 0:
-            lax.fori_loop(0, TILES - 1, pack_theta, 0, unroll=4)
-            for copy in theta_copies + theta_strip_copies(1):
-                copy.start()
-        else:
-            store.start()
-        th[3 - r, 0, own] = receive_faces(r)
-        if r == 0:
+        when(p, 0, lambda: spread_both(0, 4))
+        when(p, 1, lambda: spread_both(0, 8))
+        when(p, 2, lambda: spread_both(4, CY))
+        lax.fori_loop(by(p, 0, 3, 7), by(p, 4, 8, CY), plane_coefficients, 0)
+        sweeps(0, p, ((0, 2), (0, 1), (0, 1)), ((1, 4), (1, 3), (0, 2)), ((3, 8), (3, 8), (2, 8)))
+
+        @pl.when(p == 0)
+        def _():
+            pl.semaphore_wait(known.at[1], len(line_y))
+            send_faces(0, 3)
+
+        @pl.when(p == 1)
+        def _():
+            send_theta(0)
+            th[3, 0, own] = receive_faces(0)
+            pack_wall(1, 3)
             for copy in wall_copies(1, 3):
                 copy.start()
 
-    for r in range(ITERS):
-        iteration(r)
+        return carry
+
+    lax.fori_loop(0, 3, first_iteration, 0)
+
+    send_theta(1)
+    for copy in theta_copies(0):
+        copy.wait()
+    unpack(unpack_theta, 0, LOW)
+    for copy in wall_copies(1, 3):
+        copy.wait()
+    wall_strip(1)
+
+    def second_iteration(p, carry):
+        @pl.when(p == 1)
+        def _():
+            for copy in theta_copies(1):
+                copy.wait()
+            unpack(unpack_theta, LOW, CY)
+
+        theta_strips(p)
+        lax.fori_loop(0, 2 * SWEEPS, strip_sweep, 0)
+        when(p, 0, lambda: spread_both(0, 4))
+        when(p, 1, lambda: spread_both(0, CY))
+        sweeps(1, p, ((0, 2), (0, 1), (0, 1)), ((1, 8), (1, 8), (0, 8)))
+
+        @pl.when(p == 0)
+        def _():
+            send_faces(1, 2)
+
+        return carry
+
+    lax.fori_loop(0, 2, second_iteration, 0)
+    store.start()
+    th[2, 0, own] = receive_faces(1)
     wall_out[0] = th[2, 0, own]
     store.wait()
+
+
+def publish(theta, wall, theta_out, wall_out, field, rows, come, go):
+    half = pl.ds(0, CY // 2), pl.ds(CY // 2, CY // 2)
+    parts = [(theta.at[0, at], field.at[at], theta_out.at[0, at]) for at in half]
+    parts.append((wall.at[0], rows, wall_out.at[0]))
+    take = [pltpu.make_async_copy(source, here, come.at[i]) for i, (source, here, _) in enumerate(parts)]
+    give = [pltpu.make_async_copy(here, target, go.at[i]) for i, (_, here, target) in enumerate(parts)]
+    for copy in take:
+        copy.start()
+    for first, second in zip(take, give):
+        first.wait()
+        second.start()
+    for copy in give:
+        copy.wait()
 
 
 def solution(mesh):
@@ -479,7 +628,7 @@
         anywhere = pl.BlockSpec(memory_space=pl.ANY)
         vmem = pl.BlockSpec(memory_space=pltpu.VMEM)
         buf = lambda *shape: pltpu.VMEM(shape, F32)
-        return pl.pallas_call(
+        held = pl.pallas_call(
             functools.partial(kernel, n),
             out_shape=(
                 jax.ShapeDtypeStruct(theta.shape, F32),
@@ -501,15 +650,21 @@
                 buf(2, CY, ROWS, LZ),
                 buf(2, 2, CY, 8, LZ),
                 buf(2, 2, CY, 8, LZ),
-                buf(5, CX, LZ),
-                buf(3, CX, LZ),
-                buf(3, CX, LZ),
-                buf(2, 3, 8, LZ),
+                buf(6, CX, LZ),
                 buf(2, CX, LZ),
                 buf(2, CX, LZ),
                 buf(2, 2, 8, LZ),
+                buf(3, 4, CX, LZ),
+                buf(3, 2, 4, 8, LZ),
+                buf(2, CX, LZ),
+                buf(2, CX, LZ),
                 buf(2, 2, 8, LZ),
                 buf(2, CX, LZ),
+                buf(2, CX, LZ),
+                buf(2, 2, 8, LZ),
+                buf(2, 8, LZ),
+                buf(2, 8, LZ),
+                buf(2, 2, 8, LZ),
                 buf(2, 2, 8, LZ),
                 buf(2, CY, 8, LZ),
                 buf(n, chunk, LZ),
@@ -522,17 +677,34 @@
                 pltpu.SemaphoreType.DMA((8,)),
                 pltpu.SemaphoreType.DMA((5,)),
                 pltpu.SemaphoreType.DMA((5,)),
+                pltpu.SemaphoreType.DMA((5,)),
+                pltpu.SemaphoreType.DMA((5,)),
+                pltpu.SemaphoreType.DMA((5,)),
+                pltpu.SemaphoreType.DMA((5,)),
                 pltpu.SemaphoreType.DMA((2, 5)),
                 pltpu.SemaphoreType.DMA((2, 5)),
                 pltpu.SemaphoreType.DMA((2, 5)),
                 pltpu.SemaphoreType.DMA((2, 5)),
                 pltpu.SemaphoreType.DMA((2,)),
                 pltpu.SemaphoreType.DMA((2,)),
+                pltpu.SemaphoreType.REGULAR((2,)),
             ],
             compiler_params=pltpu.CompilerParams(
                 collective_id=0, has_side_effects=True, vmem_limit_bytes=56 * 2**20
             ),
         )(theta, cond, vel, heat, wall, kinds, blocks, rows)
+        return pl.pallas_call(
+            publish,
+            out_shape=tuple(jax.ShapeDtypeStruct(x.shape, F32) for x in held),
+            in_specs=[anywhere] * 2,
+            out_specs=(anywhere, anywhere),
+            scratch_shapes=[
+                buf(CY, CX, LZ),
+                buf(CX, LZ),
+                pltpu.SemaphoreType.DMA((3,)),
+                pltpu.SemaphoreType.DMA((3,)),
+            ],
+        )(*held)
 
     whole = P("blk", None, None, "span")
     rows = P("blk", None, "span")

time: 60.8 us -> 55.1 us (0.906)
  local copies, waits for them, and re-layouts: 3.77 us -> 0 us
  Pallas kernels: 56.3 us -> 54.4 us
    pallas_call x1, Pallas kernels: 56.3 us -> 52.3 us  [part(): pl.pallas_call(functools.partial(kernel, n), out_shape=(jax.ShapeDtypeStr...]
    unnamed x2 -> x0, local copies, waits for them, and re-layouts: 3.77 us -> none
    pallas_call x0 -> x1, Pallas kernels: none -> 2.07 us  [part(): pl.pallas_call(publish, out_shape=tuple((jax.ShapeDtypeStruct(x.shape, F3...]
where the time goes in v2:
time: 55.1 us; the launch traced here: 55 us
  Pallas kernels  54.4 us (99%)
  between operations  0.64 us (1%)
    pallas_call x1, Pallas kernels, part(): pl.pallas_call(functools.partial(kernel, n), out_shape=(jax.ShapeDtypeStr...  52.3 us
    pallas_call x1, Pallas kernels, part(): pl.pallas_call(publish, out_shape=tuple((jax.ShapeDtypeStruct(x.shape, F3...  2.07 us

profile of v2, /device:TPU:1, one launch (start us, length us, event | category | flops | bytes accessed | tf_op | source)
XLA Modules:
  0.0 55.0 jit_solution(13767522258864691864)
XLA Ops:
  0.6 52.3 %shard_map.95 = (f32[1,16,128,128]{3,2,1,0:T(8,128)}, f32[1,128,128]{2,1,0:T(8,128)}) custom-call(f32[1,16,128,128]{3,2,1,0:T(8,128)} %theta_ref.1, f32[1,16,128,128]{3,2,1,0:T(8,128)} %cond_ref.1, f32[1,3,16,128,128]{4,3,2,1,0:T(8,128)} %vel_ref.1, f32[1,16,128,128]{3,2,1,0:T(8,128)} %heat_ref.1, f32[1,128,128]{2,1,0:T(8,128)} %wall_ref.1, s32[128]{0:T(128)} %kind_ref.1, ...), custom_call_target="tpu_custom_call" | custom-call | tf_op jit(solution)/shard_map/pallas_call | solution.py:631
  52.9 2.1 %shard_map.96 = (f32[1,16,128,128]{3,2,1,0:T(8,128)}, f32[1,128,128]{2,1,0:T(8,128)}) custom-call(f32[1,16,128,128]{3,2,1,0:T(8,128)} %get-tuple-element.4.theta, f32[1,128,128]{2,1,0:T(8,128)} %get-tuple-element.5.wall), custom_call_target="tpu_custom_call" | custom-call | tf_op jit(solution)/shard_map/pallas_call | solution.py:696

commit v3 on v2

--- a/solution.py
+++ b/solution.py
@@ -48,9 +48,9 @@
     n, theta_ref, cond_ref, vel_ref, heat_ref, wall_ref, kind_ref, block_ref, row_ref,
     theta_out, wall_out,
     th, kb, vb, hb, co, st, sk, sv, sco, sw, pz,
-    xs, xr, qo, qs, qr, cr, qx, cx, qa, qar, ca, qt, qtr, ct, qw, qwr, wx, wc, tr,
+    xs, xr, qo, hq, qs, qr, cr, qx, cx, qa, qar, ca, qt, qtr, ct, qw, qwr, wx, wc, tr,
     sb, rb, choose_send, choose_recv, kinds, blocks, rows,
-    load_sem, low_send, low_recv, mid_send, mid_recv, rest_send, rest_recv, wall_send, wall_recv, theta_send, theta_recv,
+    load_sem, low_send, low_recv, rest_send, rest_recv, wall_send, wall_recv, theta_send, theta_recv,
     many_send, many_recv, known,
 ):
     b, s = lax.axis_index("blk"), lax.axis_index("span")
@@ -58,6 +58,16 @@
     east, west = lax.rem(b + 1, n), lax.rem(b + n - 1, n)
     E, W, Z, ZE, ZW = (east, s), (west, s), (b, 1 - s), (east, 1 - s), (west, 1 - s)
     own, planes = pl.ds(8, CX), pl.ds(1, CY)
+
+    def line(count, stride):
+        at = lax.rem(b // stride, count)
+        return [(b + (lax.rem(at + d, count) - at) * stride, s) for d in range(1, count)]
+
+    line_z, line_x, line_y = line(n // 16, 16), line(4, 4), line(4, 1)
+    barrier = pltpu.get_barrier_semaphore()
+    beside = [E, W, Z, ZE, ZW] + line_z + line_x + line_y
+    for peer in beside:
+        pl.semaphore_signal(barrier, inc=1, device_id=peer, device_id_type=MESH)
 
     loads = [
         pltpu.make_async_copy(kind_ref, kinds, load_sem.at[5]),
@@ -74,16 +84,6 @@
 
     rb[:, pl.ds(b, 1)] = jnp.zeros((2, 1, chunk, LZ), F32)
 
-    def line(count, stride):
-        at = lax.rem(b // stride, count)
-        return [(b + (lax.rem(at + d, count) - at) * stride, s) for d in range(1, count)]
-
-    line_z, line_x, line_y = line(n // 16, 16), line(4, 4), line(4, 1)
-    barrier = pltpu.get_barrier_semaphore()
-    beside = [E, W, Z, ZE, ZW] + line_z + line_x + line_y
-    for peer in beside:
-        pl.semaphore_signal(barrier, inc=1, device_id=peer, device_id_type=MESH)
-
     lane = lax.broadcasted_iota(jnp.int32, (8, LZ), 1)
     sub = lax.broadcasted_iota(jnp.int32, (8, LZ), 0)
     group, place = lane // 8, lane % 8
@@ -109,37 +109,49 @@
             out = jnp.where(group == y, pltpu.roll(load(y), (8 * y + 4) % LZ, 1), out)
         return out
 
-    def pack_static(at, at_pad):
-        q_k = edges(lambda y: kb[y, at_pad])
-        q_v = [edges(lambda y, d=d: vb[d, y, at]) for d in range(3)]
-        q_h = edges(lambda y: hb[y, at])
+    def pack_static(at, at_pad, count=CY):
+        q_k = edges(lambda y: kb[y, at_pad], count)
+        q_v = [edges(lambda y, d=d: vb[d, y, at], count) for d in range(3)]
+        q_h = edges(lambda y: hb[y, at], count)
         return [q_k] + q_v + [q_h]
+
+    def beside_middle(x):
+        return jnp.where(place >= 6, pltpu.roll(x, 4, 1), pltpu.roll(x, LZ - 4, 1))
+
+    def from_beside(x):
+        return jnp.where(low_half, pltpu.roll(x, LZ - 4, 1), pltpu.roll(x, 4, 1))
 
     def paired(q):
         return [
             q[0],
-            jnp.where(middle, q[1], pltpu.roll(q[2], 4, 1)),
-            jnp.where(middle, q[3], pltpu.roll(q[4], 4, 1)),
+            jnp.where(middle, q[1], beside_middle(q[2])),
+            jnp.where(middle, q[3], beside_middle(q[4])),
         ]
+
+    def pack_low(i, carry):
+        at = pl.ds(pl.multiple_of(8 * i, 8), 8)
+        at_pad = pl.ds(pl.multiple_of(8 * i + 8, 8), 8)
+        q = pack_static(at, at_pad, LOW) + [edges(lambda y: th[0, y + 1, at_pad], LOW)]
+        sent = [q[5]] + paired(q)
+        out = sent[0]
+        for slot in range(1, 4):
+            out = jnp.where(group >= LOW * slot, pltpu.roll(sent[slot], 8 * LOW * slot, 1), out)
+        qa[at] = out
+        return carry
 
     def pack_tile(i, carry):
         at = pl.ds(pl.multiple_of(8 * i, 8), 8)
         at_pad = pl.ds(pl.multiple_of(8 * i + 8, 8), 8)
         q = pack_static(at, at_pad) + [edges(lambda y: th[0, y + 1, at_pad])]
         sent = [q[5]] + paired(q)
+        rest = [jnp.where(group < LOW, pltpu.roll(sent[3], LZ - 32 * (m + 1), 1), sent[m]) for m in range(3)]
         for slot in range(6):
             qo[slot, at] = q[slot]
-        for slot in range(2):
-            qs[slot, at] = jnp.where(group < 8, pltpu.roll(sent[2 * slot], 64, 1), sent[2 * slot + 1])
-        for half in range(2):
-            parts = [pltpu.roll(q, (32 * (slot - half)) % LZ, 1) if slot != half else q for slot, q in enumerate(sent)]
-            out = parts[0]
-            for slot in range(1, 4):
-                out = jnp.where(group >= 4 * slot, parts[slot], out)
-            qa[half, at] = out
+        for slot in range(3):
+            qs[slot, at] = rest[slot]
         return carry
 
-    lax.fori_loop(0, TILES - 1, pack_tile, 0, unroll=2)
+    lax.fori_loop(0, TILES - 1, pack_low, 0, unroll=4)
 
     def pack_rows(y, carry):
         end, pad_end = pl.ds(CX - 8, 8), pl.ds(CX, 8)
@@ -192,7 +204,7 @@
         ]
 
     head, tail = pl.ds(0, 8), pl.ds(CX - 8, 8)
-    low, mid, rest = pl.ds(0, LOW), pl.ds(LOW, LOW), pl.ds(2 * LOW, CY - 2 * LOW)
+    low, rest = pl.ds(0, LOW), pl.ds(LOW, CY - LOW)
 
     def theta_copies(late):
         ss, rs = theta_send.at[late], theta_recv.at[late]
@@ -205,17 +217,13 @@
             remote(qt.at[late], qtr.at[late], ss.at[0], rs.at[0], Z),
         ]
 
-    def part_copies(half, planes, ss, rs):
-        return [
-            remote(qa.at[half, tail], ca.at[half, 0], ss.at[3], rs.at[3], ZE),
-            remote(qa.at[half, head], ca.at[half, 1], ss.at[4], rs.at[4], ZW),
-            remote(xs.at[0, :, planes], xr.at[0, :, planes], ss.at[0], rs.at[0], E),
-            remote(xs.at[1, :, planes], xr.at[1, :, planes], ss.at[1], rs.at[1], W),
-            remote(qa.at[half], qar.at[half], ss.at[2], rs.at[2], Z),
-        ]
-
-    low_copies = part_copies(0, low, low_send, low_recv)
-    mid_copies = part_copies(1, mid, mid_send, mid_recv)
+    low_copies = [
+        remote(qa.at[tail], ca.at[0], low_send.at[3], low_recv.at[3], ZE),
+        remote(qa.at[head], ca.at[1], low_send.at[4], low_recv.at[4], ZW),
+        remote(xs.at[0, :, low], xr.at[0, :, low], low_send.at[0], low_recv.at[0], E),
+        remote(xs.at[1, :, low], xr.at[1, :, low], low_send.at[1], low_recv.at[1], W),
+        remote(qa, qar, low_send.at[2], low_recv.at[2], Z),
+    ]
     rest_copies = [
         remote(qs.at[:, tail], cr.at[0], rest_send.at[3], rest_recv.at[3], ZE),
         remote(qs.at[:, head], cr.at[1], rest_send.at[4], rest_recv.at[4], ZW),
@@ -224,6 +232,10 @@
         remote(qs, qr, rest_send.at[2], rest_recv.at[2], Z),
     ]
     for copy in low_copies + wall_copies(0, 0):
+        copy.start()
+
+    lax.fori_loop(0, TILES - 1, pack_tile, 0, unroll=2)
+    for copy in rest_copies:
         copy.start()
 
     mine = jnp.broadcast_to(blocks[...].astype(F32), (CX, CX))
@@ -243,14 +255,6 @@
         lax.broadcasted_iota(jnp.int32, (CX, 2 * CX), 1) == code_t, 1.0, 0.0
     ).astype(jnp.bfloat16)
 
-    for copy in mid_copies + rest_copies:
-        copy.start()
-    for copy in low_copies:
-        copy.wait()
-    pl.semaphore_wait(known.at[0], len(line_x))
-    for peer in line_y:
-        pl.semaphore_signal(known.at[1], inc=1, device_id=peer, device_id_type=MESH)
-
     rows_last = row8(last)
 
     def unpack_rows(y, carry):
@@ -278,45 +282,42 @@
         for slot in range(2):
             t = other_q[1 + slot]
             put_strip(sv.at[2 * slot], at, own_q[1 + 2 * slot], t)
-            put_strip(sv.at[2 * slot + 1], at, own_q[2 + 2 * slot], pltpu.roll(t, LZ - 4, 1))
-
-    def split(half, value, before):
-        parts = [pltpu.roll(value, (32 * (half - slot)) % LZ, 1) if slot != half else value for slot in range(4)]
-        return [jnp.where(group < LOW, x, y) for x, y in zip(before, parts)] if half else parts
-
-    def split_strips(half):
+            put_strip(sv.at[2 * slot + 1], at, own_q[2 + 2 * slot], from_beside(t))
+
+    def split(value):
+        return [pltpu.roll(value, LZ - 32 * slot, 1) if slot else value for slot in range(4)]
+
+    def join(value, before):
+        out = [jnp.where(group < LOW, x, y) for x, y in zip(before, value)]
+        fourth = before[3]
+        for m in range(3):
+            fourth = jnp.where(group >= LOW * (m + 1), pltpu.roll(value[m], 32 * (m + 1), 1), fourth)
+        return out + [fourth]
+
+    def take_strips(late):
         def one(i, carry):
             at = pl.ds(pl.multiple_of(8 * i, 8), 8)
-            before = [qx[0, slot, at] for slot in range(4)] if half else None
-            for slot, value in enumerate(split(half, qar[half, at], before)):
-                qx[half, slot, at] = value
+            if late:
+                out = join([qr[m, at] for m in range(3)], [qx[0, slot, at] for slot in range(4)])
+            else:
+                out = split(qar[at])
+            for slot, value in enumerate(out):
+                qx[late, slot, at] = value
             return carry
 
         lax.fori_loop(0, TILES - 1, one, 0, unroll=4)
         for side in range(2):
-            before = [cx[0, side, slot] for slot in range(4)] if half else None
-            for slot, value in enumerate(split(half, ca[half, side], before)):
-                cx[half, side, slot] = value
-
-    def join_rest(value, before):
-        return [
-            jnp.where(group < 8, x, pltpu.roll(value[slot // 2], 64, 1) if slot % 2 == 0 else value[slot // 2])
-            for slot, x in enumerate(before)
-        ]
-
-    def join_strips():
-        def one(i, carry):
-            at = pl.ds(pl.multiple_of(8 * i, 8), 8)
-            all_planes = join_rest([qr[slot, at] for slot in range(2)], [qx[1, slot, at] for slot in range(4)])
-            for slot, value in enumerate(all_planes):
-                qx[2, slot, at] = value
-            return carry
-
-        lax.fori_loop(0, TILES - 1, one, 0, unroll=4)
-        for side in range(2):
-            all_planes = join_rest([cr[side, slot] for slot in range(2)], [cx[1, side, slot] for slot in range(4)])
-            for slot, value in enumerate(all_planes):
-                cx[2, side, slot] = value
+            if late:
+                out = join([cr[side, m] for m in range(3)], [cx[0, side, slot] for slot in range(4)])
+            else:
+                out = split(ca[side])
+            for slot, value in enumerate(out):
+                cx[late, side, slot] = value
+
+    def pack_halo(count):
+        q = pack_static(rows_last, tile(last), count) + [edges(lambda y: th[0, y + 1, tile(last)], count)]
+        for slot in range(6):
+            hq[slot] = q[slot]
 
     def static_strips(late):
         def one(i, carry):
@@ -328,8 +329,8 @@
 
         lax.fori_loop(0, TILES - 1, one, 0, unroll=4)
         other = [jnp.where(near, cx[late, 1, slot], cx[late, 0, slot]) for slot in range(4)]
-        put_strip(st.at[0], tile(last), edges(lambda y: th[0, y + 1, tile(last)]), other[0])
-        put_static(rows_last, tile(last), pack_static(rows_last, tile(last)), other[1:])
+        put_strip(st.at[0], tile(last), hq[5], other[0])
+        put_static(rows_last, tile(last), [hq[slot] for slot in range(5)], other[1:])
         wrap(st.at[0])
         wrap(sk)
 
@@ -355,42 +356,59 @@
     strip_group = lax.broadcasted_iota(jnp.int32, (ROWS, LZ), 1) // 8
     strip_first = strip_group == 0
 
-    def strip_coefficients(side, carry):
-        k = sk[side, whole]
-        a = coefficients(
-            k, sk[side, whole_w], sk[side, whole_e], pltpu.roll(k, 1, 1), pltpu.roll(k, LZ - 1, 1),
-            jnp.where(strip_first, k, pltpu.roll(k, 8, 1)), pltpu.roll(k, LZ - 8, 1), [sv[d, side] for d in range(3)],
-            lambda x: jnp.where(strip_row == 0, same_west * x, x),
-            lambda x: jnp.where(strip_row == CX - 1, same_east * x, x),
-            strip_first.astype(F32), (strip_group == CY - 1).astype(F32),
-        )
-        for slot, value in enumerate(a):
-            sco[slot, side] = value
-        return carry
-
-    def plane_coefficients(y, carry):
-        bottom = (y == 0).astype(F32)
-        top = (y == CY - 1).astype(F32)
-        below, above = jnp.maximum(y - 1, 0), jnp.minimum(y + 1, CY - 1)
-        for i in range(TILES):
-            k = kb[y, tile(i)]
-            k_s, k_n = pltpu.roll(k, 1, 1), pltpu.roll(k, LZ - 1, 1)
-            mask_w = (lambda x: jnp.where(sub == 0, same_west * x, x)) if i == 0 else (lambda x: x)
-            mask_e = (lambda x: jnp.where(sub == 7, same_east * x, x)) if i == last - 1 else (lambda x: x)
-            a = coefficients(
-                k, kb[y, tile(i, -1)], kb[y, tile(i, 1)], k_s, k_n, kb[below, tile(i)], kb[above, tile(i)],
-                [vb[d, y, row8(i)] for d in range(3)], mask_w, mask_e, bottom, top,
-            )
+    def strip_coefficients():
+        both = []
+        for side in range(2):
+            k = sk[side, whole]
+            both.append(coefficients(
+                k, sk[side, whole_w], sk[side, whole_e], pltpu.roll(k, 1, 1), pltpu.roll(k, LZ - 1, 1),
+                jnp.where(strip_first, k, pltpu.roll(k, 8, 1)), pltpu.roll(k, LZ - 8, 1),
+                [sv[d, side] for d in range(3)],
+                lambda x: jnp.where(strip_row == 0, same_west * x, x),
+                lambda x: jnp.where(strip_row == CX - 1, same_east * x, x),
+                strip_first.astype(F32), (strip_group == CY - 1).astype(F32),
+            ))
+        for side, a in enumerate(both):
             for slot, value in enumerate(a):
-                co[slot, y, row8(i)] = value
-        return carry
+                sco[slot, side] = value
+
+    def plane_coefficients(tiles):
+        def one(y, carry):
+            bottom = (y == 0).astype(F32)
+            top = (y == CY - 1).astype(F32)
+            below, above = jnp.maximum(y - 1, 0), jnp.minimum(y + 1, CY - 1)
+            for i in tiles:
+                k = kb[y, tile(i)]
+                k_s, k_n = pltpu.roll(k, 1, 1), pltpu.roll(k, LZ - 1, 1)
+                mask_w = (lambda x: jnp.where(sub == 0, same_west * x, x)) if i == 0 else (lambda x: x)
+                mask_e = (lambda x: jnp.where(sub == 7, same_east * x, x)) if i == last - 1 else (lambda x: x)
+                a = coefficients(
+                    k, kb[y, tile(i, -1)], kb[y, tile(i, 1)], k_s, k_n, kb[below, tile(i)], kb[above, tile(i)],
+                    [vb[d, y, row8(i)] for d in range(3)], mask_w, mask_e, bottom, top,
+                )
+                for slot, value in enumerate(a):
+                    co[slot, y, row8(i)] = value
+            return carry
+
+        return one
+
+    inner = plane_coefficients(range(1, last - 1))
+    outer = plane_coefficients((0, last - 1, last))
+
+    lax.fori_loop(0, CY, inner, 0, unroll=2)
+
+    for copy in low_copies:
+        copy.wait()
+    pl.semaphore_wait(known.at[0], len(line_x))
+    for peer in line_y:
+        pl.semaphore_signal(known.at[1], inc=1, device_id=peer, device_id_type=MESH)
 
     edge_two, edge_one = (lane < 2) | (lane >= LZ - 2), first_lane | last_lane
 
-    def sweep(t, following, step, first, end):
-        def pair(g, carry):
-            for half in range(2):
-                y = 2 * g + half
+    def sweep(t, following, step, first, end, size):
+        def some(g, carry):
+            for m in range(size):
+                y = size * g + m
                 for i in range(TILES):
                     at = row8(i)
                     c = th[t, y + 1, tile(i)]
@@ -409,22 +427,28 @@
                         th[following, y + 1, tile(TILES)] = new
             return carry
 
-        lax.fori_loop(first, end, pair, 0)
-
-    def strip_sweep(m, carry):
-        step, side = m // 2, m % 2
-        c = st[step, side, whole]
-        below = jnp.where(strip_first, sw[side], pltpu.roll(c, 8, 1))
-        new = (
-            (sv[3, side] + sco[AD, side] * c)
-            + (sco[AW, side] * st[step, side, whole_w] + sco[AE, side] * st[step, side, whole_e])
-            + (sco[AS, side] * pltpu.roll(c, 1, 1) + sco[AN, side] * pltpu.roll(c, LZ - 1, 1))
-            + (sco[AB, side] * below + sco[AA, side] * pltpu.roll(c, LZ - 8, 1))
-        )
-        st[step + 1, side, whole] = new
-        st[step + 1, side, tile(-1)] = new[ROWS - 8 :]
-        st[step + 1, side, tile(TILES)] = new[:8]
-        return carry
+        lax.fori_loop(first, end, some, 0)
+
+    first_group = group == 0
+
+    def strip_sweeps():
+        for step in range(SWEEPS):
+            for side in range(2):
+                for i in range(TILES):
+                    at = row8(i)
+                    c = st[step, side, tile(i)]
+                    below = jnp.where(first_group, sw[side, at], pltpu.roll(c, 8, 1))
+                    new = (
+                        (sv[3, side, at] + sco[AD, side, at] * c)
+                        + (sco[AW, side, at] * st[step, side, tile(i, -1)] + sco[AE, side, at] * st[step, side, tile(i, 1)])
+                        + (sco[AS, side, at] * pltpu.roll(c, 1, 1) + sco[AN, side, at] * pltpu.roll(c, LZ - 1, 1))
+                        + (sco[AB, side, at] * below + sco[AA, side, at] * pltpu.roll(c, LZ - 8, 1))
+                    )
+                    st[step + 1, side, tile(i)] = new
+                    if i == last:
+                        st[step + 1, side, tile(-1)] = new
+                    if i == 0:
+                        st[step + 1, side, tile(TILES)] = new
 
     def spread(slot, first, end):
         strips = [jnp.where(low_half, st[slot + 2, 1, tile(i)], st[slot + 2, 0, tile(i)]) for i in range(TILES)]
@@ -476,7 +500,7 @@
 
         lax.fori_loop(0, TILES - 1, one, 0, unroll=4)
         put_strip(
-            st.at[0], tile(last), edges(lambda y: th[3, y + 1, tile(last)]), jnp.where(near, ct[late, 1], ct[late, 0])
+            st.at[0], tile(last), edges(lambda y: th[3, y + 1, tile(last)], CY if late else LOW), jnp.where(near, ct[late, 1], ct[late, 0])
         )
         wrap(st.at[0])
 
@@ -499,16 +523,13 @@
 
     store = pltpu.make_async_copy(th.at[2, planes, own], theta_out.at[0], load_sem.at[0])
 
-    def by(p, *values):
-        out = values[0] + p * (values[1] - values[0])
-        if len(values) == 3:
-            out = out + p * (p - 1) // 2 * (values[2] - 2 * values[1] + values[0])
-        return out
-
-    def sweeps(r, p, *bounds):
+    def early_sweeps(r):
+        for step, pairs in enumerate((2, 1, 1)):
+            sweep((3 * r + step) % 4, (3 * r + step + 1) % 4, step, 0, pairs, 2)
+
+    def late_sweeps(r):
         for step in range(SWEEPS):
-            first, end = zip(*[bound[step] for bound in bounds])
-            sweep((3 * r + step) % 4, (3 * r + step + 1) % 4, step, by(p, *first), by(p, *end))
+            sweep((3 * r + step) % 4, (3 * r + step + 1) % 4, step, 0, CY // 4, 4)
 
     def when(p, value, action):
         pl.when(p == value)(action)
@@ -527,53 +548,47 @@
     def first_iteration(p, carry):
         @pl.when(p == 0)
         def _():
-            split_strips(0)
+            take_strips(0)
             unpack(unpack_rows, 0, LOW)
+            pack_halo(LOW)
+            lax.fori_loop(0, LOW, outer, 0, unroll=4)
 
         @pl.when(p == 1)
-        def _():
-            for copy in mid_copies:
-                copy.wait()
-            split_strips(1)
-            unpack(unpack_rows, LOW, 2 * LOW)
-
-        @pl.when(p == 2)
         def _():
             for copy in rest_copies:
                 copy.wait()
-            join_strips()
-            unpack(unpack_rows, 2 * LOW, CY)
+            take_strips(1)
+            unpack(unpack_rows, LOW, CY)
+            pack_halo(CY)
+            lax.fori_loop(0, CY, outer, 0, unroll=4)
 
         static_strips(p)
-        lax.fori_loop(0, 2, strip_coefficients, 0)
-        lax.fori_loop(0, 2 * SWEEPS, strip_sweep, 0)
+        strip_coefficients()
+        strip_sweeps()
         when(p, 0, lambda: spread_both(0, 4))
-        when(p, 1, lambda: spread_both(0, 8))
-        when(p, 2, lambda: spread_both(4, CY))
-        lax.fori_loop(by(p, 0, 3, 7), by(p, 4, 8, CY), plane_coefficients, 0)
-        sweeps(0, p, ((0, 2), (0, 1), (0, 1)), ((1, 4), (1, 3), (0, 2)), ((3, 8), (3, 8), (2, 8)))
+        when(p, 1, lambda: spread_both(0, CY))
+        when(p, 0, lambda: early_sweeps(0))
+        when(p, 1, lambda: late_sweeps(0))
 
         @pl.when(p == 0)
         def _():
             pl.semaphore_wait(known.at[1], len(line_y))
             send_faces(0, 3)
 
-        @pl.when(p == 1)
-        def _():
-            send_theta(0)
-            th[3, 0, own] = receive_faces(0)
-            pack_wall(1, 3)
-            for copy in wall_copies(1, 3):
-                copy.start()
-
         return carry
 
-    lax.fori_loop(0, 3, first_iteration, 0)
-
+    lax.fori_loop(0, 2, first_iteration, 0)
+
+    send_theta(0)
+    th[3, 0, own] = receive_faces(0)
+    pack_wall(1, 3)
+    for copy in wall_copies(1, 3):
+        copy.start()
     send_theta(1)
     for copy in theta_copies(0):
         copy.wait()
     unpack(unpack_theta, 0, LOW)
+    theta_strips(0)
     for copy in wall_copies(1, 3):
         copy.wait()
     wall_strip(1)
@@ -584,12 +599,13 @@
             for copy in theta_copies(1):
                 copy.wait()
             unpack(unpack_theta, LOW, CY)
-
-        theta_strips(p)
-        lax.fori_loop(0, 2 * SWEEPS, strip_sweep, 0)
+            theta_strips(1)
+
+        strip_sweeps()
         when(p, 0, lambda: spread_both(0, 4))
         when(p, 1, lambda: spread_both(0, CY))
-        sweeps(1, p, ((0, 2), (0, 1), (0, 1)), ((1, 8), (1, 8), (0, 8)))
+        when(p, 0, lambda: early_sweeps(1))
+        when(p, 1, lambda: late_sweeps(1))
 
         @pl.when(p == 0)
         def _():
@@ -651,14 +667,15 @@
                 buf(2, 2, CY, 8, LZ),
                 buf(2, 2, CY, 8, LZ),
                 buf(6, CX, LZ),
-                buf(2, CX, LZ),
-                buf(2, CX, LZ),
-                buf(2, 2, 8, LZ),
-                buf(3, 4, CX, LZ),
-                buf(3, 2, 4, 8, LZ),
-                buf(2, CX, LZ),
-                buf(2, CX, LZ),
-                buf(2, 2, 8, LZ),
+                buf(6, 8, LZ),
+                buf(3, CX, LZ),
+                buf(3, CX, LZ),
+                buf(2, 3, 8, LZ),
+                buf(2, 4, CX, LZ),
+                buf(2, 2, 4, 8, LZ),
+                buf(CX, LZ),
+                buf(CX, LZ),
+                buf(2, 8, LZ),
                 buf(2, CX, LZ),
                 buf(2, CX, LZ),
                 buf(2, 2, 8, LZ),
@@ -675,8 +692,6 @@
                 pltpu.VMEM((1, CX), jnp.int32),
                 pltpu.VMEM((1, CX), jnp.int32),
                 pltpu.SemaphoreType.DMA((8,)),
-                pltpu.SemaphoreType.DMA((5,)),
-                pltpu.SemaphoreType.DMA((5,)),
                 pltpu.SemaphoreType.DMA((5,)),
                 pltpu.SemaphoreType.DMA((5,)),
                 pltpu.SemaphoreType.DMA((5,)),

time: 55.1 us -> 48.5 us (0.88)
  Pallas kernels: 54.4 us -> 47.7 us
    pallas_call x1, Pallas kernels: 52.3 us -> 45.7 us  [part(): pl.pallas_call(functools.partial(kernel, n), out_shape=(jax.ShapeDtypeStr...]
where the time goes in v3:
time: 48.5 us; the launch traced here: 48.4 us
  Pallas kernels  47.7 us (98%)
  between operations  0.64 us (1%)
    pallas_call x1, Pallas kernels, part(): pl.pallas_call(functools.partial(kernel, n), out_shape=(jax.ShapeDtypeStr...  45.7 us
    pallas_call x1, Pallas kernels, part(): pl.pallas_call(publish, out_shape=tuple((jax.ShapeDtypeStruct(x.shape, F3...  2.07 us

profile of v3, /device:TPU:1, one launch (start us, length us, event | category | flops | bytes accessed | tf_op | source)
XLA Modules:
  0.0 48.4 jit_solution(3767705840872431633)
XLA Ops:
  0.6 45.7 %shard_map.95 = (f32[1,16,128,128]{3,2,1,0:T(8,128)}, f32[1,128,128]{2,1,0:T(8,128)}) custom-call(f32[1,16,128,128]{3,2,1,0:T(8,128)} %theta_ref.1, f32[1,16,128,128]{3,2,1,0:T(8,128)} %cond_ref.1, f32[1,3,16,128,128]{4,3,2,1,0:T(8,128)} %vel_ref.1, f32[1,16,128,128]{3,2,1,0:T(8,128)} %heat_ref.1, f32[1,128,128]{2,1,0:T(8,128)} %wall_ref.1, s32[128]{0:T(128)} %kind_ref.1, ...), custom_call_target="tpu_custom_call" | custom-call | tf_op jit(solution)/shard_map/pallas_call | solution.py:647
  46.3 2.1 %shard_map.96 = (f32[1,16,128,128]{3,2,1,0:T(8,128)}, f32[1,128,128]{2,1,0:T(8,128)}) custom-call(f32[1,16,128,128]{3,2,1,0:T(8,128)} %get-tuple-element.4.theta, f32[1,128,128]{2,1,0:T(8,128)} %get-tuple-element.5.wall), custom_call_target="tpu_custom_call" | custom-call | tf_op jit(solution)/shard_map/pallas_call | solution.py:711

commit v4 on v3

--- a/solution.py
+++ b/solution.py
@@ -294,7 +294,7 @@
             fourth = jnp.where(group >= LOW * (m + 1), pltpu.roll(value[m], 32 * (m + 1), 1), fourth)
         return out + [fourth]
 
-    def take_strips(late):
+    def take_tiles(late):
         def one(i, carry):
             at = pl.ds(pl.multiple_of(8 * i, 8), 8)
             if late:
@@ -306,6 +306,8 @@
             return carry
 
         lax.fori_loop(0, TILES - 1, one, 0, unroll=4)
+
+    def take_sides(late):
         for side in range(2):
             if late:
                 out = join([cr[side, m] for m in range(3)], [cx[0, side, slot] for slot in range(4)])
@@ -319,7 +321,7 @@
         for slot in range(6):
             hq[slot] = q[slot]
 
-    def static_strips(late):
+    def static_tiles(late):
         def one(i, carry):
             at = pl.ds(pl.multiple_of(8 * i, 8), 8)
             at_pad = pl.ds(pl.multiple_of(8 * i + 8, 8), 8)
@@ -328,6 +330,8 @@
             return carry
 
         lax.fori_loop(0, TILES - 1, one, 0, unroll=4)
+
+    def static_halo(late):
         other = [jnp.where(near, cx[late, 1, slot], cx[late, 0, slot]) for slot in range(4)]
         put_strip(st.at[0], tile(last), hq[5], other[0])
         put_static(rows_last, tile(last), [hq[slot] for slot in range(5)], other[1:])
@@ -397,7 +401,10 @@
 
     lax.fori_loop(0, CY, inner, 0, unroll=2)
 
-    for copy in low_copies:
+    low_copies[4].wait()
+    take_tiles(0)
+    static_tiles(0)
+    for copy in low_copies[:4]:
         copy.wait()
     pl.semaphore_wait(known.at[0], len(line_x))
     for peer in line_y:
@@ -548,7 +555,7 @@
     def first_iteration(p, carry):
         @pl.when(p == 0)
         def _():
-            take_strips(0)
+            take_sides(0)
             unpack(unpack_rows, 0, LOW)
             pack_halo(LOW)
             lax.fori_loop(0, LOW, outer, 0, unroll=4)
@@ -557,12 +564,14 @@
         def _():
             for copy in rest_copies:
                 copy.wait()
-            take_strips(1)
+            take_tiles(1)
+            take_sides(1)
+            static_tiles(1)
             unpack(unpack_rows, LOW, CY)
             pack_halo(CY)
             lax.fori_loop(0, CY, outer, 0, unroll=4)
 
-        static_strips(p)
+        static_halo(p)
         strip_coefficients()
         strip_sweeps()
         when(p, 0, lambda: spread_both(0, 4))

time: 48.5 us -> 48.4 us (level)
  no operation moved by 1% of the time
where the time goes in v4:
time: 48.4 us; the launch traced here: 48.3 us
  Pallas kernels  47.7 us (99%)
  between operations  0.64 us (1%)
    pallas_call x1, Pallas kernels, part(): pl.pallas_call(functools.partial(kernel, n), out_shape=(jax.ShapeDtypeStr...  45.6 us
    pallas_call x1, Pallas kernels, part(): pl.pallas_call(publish, out_shape=tuple((jax.ShapeDtypeStruct(x.shape, F3...  2.07 us

profile of v4, /device:TPU:1, one launch (start us, length us, event | category | flops | bytes accessed | tf_op | source)
XLA Modules:
  0.0 48.3 jit_solution(1449241980365309474)
XLA Ops:
  0.6 45.6 %shard_map.95 = (f32[1,16,128,128]{3,2,1,0:T(8,128)}, f32[1,128,128]{2,1,0:T(8,128)}) custom-call(f32[1,16,128,128]{3,2,1,0:T(8,128)} %theta_ref.1, f32[1,16,128,128]{3,2,1,0:T(8,128)} %cond_ref.1, f32[1,3,16,128,128]{4,3,2,1,0:T(8,128)} %vel_ref.1, f32[1,16,128,128]{3,2,1,0:T(8,128)} %heat_ref.1, f32[1,128,128]{2,1,0:T(8,128)} %wall_ref.1, s32[128]{0:T(128)} %kind_ref.1, ...), custom_call_target="tpu_custom_call" | custom-call | tf_op jit(solution)/shard_map/pallas_call | solution.py:656
  46.3 2.1 %shard_map.96 = (f32[1,16,128,128]{3,2,1,0:T(8,128)}, f32[1,128,128]{2,1,0:T(8,128)}) custom-call(f32[1,16,128,128]{3,2,1,0:T(8,128)} %get-tuple-element.4.theta, f32[1,128,128]{2,1,0:T(8,128)} %get-tuple-element.5.wall), custom_call_target="tpu_custom_call" | custom-call | tf_op jit(solution)/shard_map/pallas_call | solution.py:720
